TPU v7x, 768 devices: a whole 4x8x12 slice. The times are simulated.
768 devices in a mesh: db: 64 (over y, x, core), mp: 12 (over z).
Axes of the slice: x: 4, y: 8, z: 12, core: 2. Of those that a mesh axis runs over, the one named last changes fastest.
Arguments:
- hidden: bfloat16 [49152, 4096], P(('db', 'mp')), may hold values from -6 to 6
- norm_gain: float32 [4096], replicated, may hold values from 0.25 to 1.75
- query_weight: bfloat16 [4096, 3072], P(None, 'mp'), may hold values from -0.09375 to 0.09375
- key_weight: bfloat16 [4096, 3072], P(None, 'mp'), may hold values from -0.09375 to 0.09375
- value_weight: bfloat16 [4096, 3072], P(None, 'mp'), may hold values from -0.09375 to 0.09375
- bank: bfloat16 [256, 128, 4096], P('db'), may hold values from -6 to 6
- neighbour_ids: int32 [768, 2], P('db'), may hold values from 0 to 255, as said below
Outputs:
- attended: bfloat16 [49152, 3072], P('db', 'mp')
Inputs may be any that keep to these rules, and one draw needn't show every extreme that they name: `neighbour_ids`: the 12 rows of one db index name at most 1 ids in the range of any one shard (ids j*4 to (j+1)*4 - 1), and exactly 1 in some shard.
All inputs are finite; a program needn't handle non-finite values.
Results may differ from a plain program's by a relative error of at most 0.025.
Values may be sent and summed in bfloat16 or wider, within the bound.
A program may use at most 64 MiB of HBM per device.

v0:
```python
import jax
import jax.numpy as jnp
from jax import lax
from jax.sharding import PartitionSpec as P

HD = 128
BLOCK = 64
NBR_LEN = 128


def per_device(hidden, norm_gain, query_weight, key_weight, value_weight, bank, neighbour_ids):
    local_width = query_weight.shape[1]
    heads_here = local_width // HD
    blocks_here = neighbour_ids.shape[0]
    pairs = neighbour_ids.shape[1]
    requests = blocks_here * pairs
    shards = lax.axis_size("db")
    room = (requests + shards - 1) // shards
    slot_count = shards * room
    bank_rows = bank.shape[0]
    scale = HD ** (-0.5)
    stream = hidden.astype(jnp.float32)
    factor = lax.rsqrt(jnp.mean(stream * stream, axis=-1, keepdims=True) + 1e-06)
    queries = (
        jnp.dot(
            lax.all_gather(
                (stream * factor * norm_gain).astype(jnp.bfloat16), "mp", axis=0, tiled=True
            ),
            query_weight,
            preferred_element_type=jnp.float32,
        )
        * scale
    ).astype(jnp.bfloat16)
    flat_bank = bank.reshape(bank_rows * NBR_LEN, bank.shape[2])
    bank_keys = (
        jnp.dot(flat_bank, key_weight, preferred_element_type=jnp.float32)
        .astype(jnp.bfloat16)
        .reshape(bank_rows, NBR_LEN, local_width)
    )
    bank_values = (
        jnp.dot(flat_bank, value_weight, preferred_element_type=jnp.float32)
        .astype(jnp.bfloat16)
        .reshape(bank_rows, NBR_LEN, local_width)
    )
    flat_ids = neighbour_ids.reshape(requests)
    owners = flat_ids // bank_rows
    local_row = flat_ids % bank_rows
    request_index = jnp.arange(requests, dtype=jnp.int32)
    earlier = (owners[None, :] == owners[:, None]) & (
        request_index[None, :] < request_index[:, None]
    )
    ranked = jnp.sum(earlier.astype(jnp.int32), axis=1)
    target = owners * room + ranked
    target_hit = target[None, :] == jnp.arange(slot_count, dtype=jnp.int32)[:, None]
    query_rows = jnp.repeat(queries.reshape(blocks_here, BLOCK * local_width), pairs, axis=0)
    send_queries = jnp.dot(
        target_hit.astype(jnp.bfloat16), query_rows, preferred_element_type=jnp.bfloat16
    ).reshape(shards, room, BLOCK, local_width)
    send_rows = jnp.sum(jnp.where(target_hit, local_row[None, :], 0), axis=1).reshape(shards, room)
    got_queries = lax.all_to_all(send_queries, "db", split_axis=0, concat_axis=0, tiled=True)
    got_rows = lax.all_to_all(send_rows, "db", split_axis=0, concat_axis=0, tiled=True)
    item_count = got_rows.shape[1]
    flat_rows = got_rows.reshape(-1)
    near_keys = jnp.take(bank_keys, flat_rows, axis=0)
    near_values = jnp.take(bank_values, flat_rows, axis=0)
    asking = got_queries.reshape(-1, BLOCK, local_width)
    results = []
    log_totals = []
    for serve_head_index in range(heads_here):
        serve_first_col = serve_head_index * HD
        serve_last_col = serve_first_col + HD
        scores = jnp.einsum(
            "sqd,skd->sqk",
            asking[:, :, serve_first_col:serve_last_col],
            near_keys[:, :, serve_first_col:serve_last_col],
            preferred_element_type=jnp.float32,
        )
        exponent = jnp.exp(scores)
        denom = jnp.sum(exponent, axis=-1, keepdims=True)
        log_totals.append(jnp.log(denom)[..., 0])
        probs = (exponent / denom).astype(jnp.bfloat16)
        results.append(
            jnp.einsum(
                "sqk,skd->sqd",
                probs,
                near_values[:, :, serve_first_col:serve_last_col],
                preferred_element_type=jnp.float32,
            ).astype(jnp.bfloat16)
        )
    result = jnp.concatenate(results, axis=-1).reshape(shards, item_count, BLOCK, local_width)
    lse_rows = jnp.concatenate(log_totals, axis=-1).reshape(shards, item_count, heads_here * BLOCK)
    back_result = lax.all_to_all(result, "db", split_axis=0, concat_axis=0, tiled=True)
    back_lse = lax.all_to_all(
        lse_rows.astype(jnp.bfloat16), "db", split_axis=0, concat_axis=0, tiled=True
    ).astype(lse_rows.dtype)
    parts = jnp.take(back_result.reshape(slot_count, BLOCK * local_width), target, axis=0).reshape(
        blocks_here, pairs, BLOCK, local_width
    )
    lse_all = jnp.take(back_lse.reshape(slot_count, heads_here * BLOCK), target, axis=0).reshape(
        blocks_here, pairs, heads_here, BLOCK
    )
    total = jnp.log(jnp.sum(jnp.exp(lse_all), axis=1, keepdims=True))
    weights = jnp.exp(lse_all - total)
    outputs = []
    for head_index in range(heads_here):
        first_col = head_index * HD
        last_col = first_col + HD
        weighted = weights[:, :, head_index, :, None] * parts[:, :, :, first_col:last_col].astype(
            jnp.float32
        )
        outputs.append(jnp.sum(weighted, axis=1))
    attended = (
        jnp.concatenate(outputs, axis=-1)
        .astype(jnp.bfloat16)
        .reshape(blocks_here * BLOCK, local_width)
    )
    return attended


def solution(mesh):
    placed = (
        P(("db", "mp"), None),
        P(),
        P(None, "mp"),
        P(None, "mp"),
        P(None, "mp"),
        P("db", None, None),
        P("db", None),
    )
    return jax.shard_map(
        per_device, mesh=mesh, in_specs=placed, out_specs=P("db", "mp"), check_vma=False
    )
```

profile of v0, /device:TPU:1, one launch (start us, length us, event | category | flops | bytes accessed | tf_op | source)
XLA Modules:
  0.0 271.5 jit_solution(1376047244576655923)
XLA Ops:
  6.5 1.4 fusion.15
  8.0 2.0 fusion.17
  11.2 14.5 %all-to-all-start.1 = ((s32[64,1,1]{2,1,0:T(1,128)}), s32[64,1,1]{2,1,0:T(1,128)S(1)}, u32[]{:S(2)}, u32[]{:S(2)}) async-start(s32[64,1,1]{2,1,0:T(1,128)} %copy.55), calls=%async_computation.1 | async-start | bytes 65536 | tf_op jit(solution)/shard_map/all_to_all | solution.py:61
  25.8 76.4 %all-gather.2.cloned.1.call-done = bf16[768,4096]{1,0:T(8,128)(2,1)} async-done(((bf16[64,4096]{1,0:T(8,128)(2,1)}), bf16[768,4096]{1,0:T(8,128)(2,1)}) %all-gather.2.cloned.1.call-update) | async-done | bytes 6291472 | tf_op jit(solution)/shard_map/all_gather | solution.py:26
  102.2 4.6 %fusion.14 = bf16[768,256]{1,0:T(8,128)(2,1)S(1)} fusion(bf16[768,4096]{1,0:T(8,128)(2,1)} %all-gather.2.cloned.1.call-done, bf16[4096,256]{1,0:T(8,128)(2,1)S(1)} %copy-done), kind=kOutput, calls=%fused_computation.25 | convolution fusion | flops 1611005952 | bytes 8781824 | tf_op jit(solution)/shard_map/dot_general | solution.py:25
  108.9 2.0 convolution_bitcast_fusion
  110.8 2.5 copy.54
  113.3 10.6 %all-to-all-start = ((bf16[64,1,64,256]{3,2,1,0:T(8,128)(2,1)}), bf16[64,1,64,256]{3,2,1,0:T(8,128)(2,1)}, u32[]{:S(2)}, u32[]{:S(2)}) async-start(bf16[64,1,64,256]{3,2,1,0:T(8,128)(2,1)} %copy.54), calls=%async_computation | async-start | bytes 4194304 | tf_op jit(solution)/shard_map/all_to_all | solution.py:60
  123.9 4.3 %convolution_convert_fusion.1 = bf16[512,256]{1,0:T(8,128)(2,1)S(1)} fusion(bf16[512,4096]{1,0:T(8,128)(2,1)} %bitcast.59, bf16[4096,256]{1,0:T(8,128)(2,1)} %param.12), kind=kOutput, calls=%fused_computation.27 | convolution fusion | flops 1073872896 | bytes 6553600 | tf_op jit(solution)/shard_map/dot_general | solution.py:36
  128.6 1.2 convolution_convert_fusion
  131.1 2.7 %gather_fusion.3 = bf16[64,128,256]{2,1,0:T(8,128)(2,1)} fusion(bf16[4,128,256]{2,1,0:T(8,128)(2,1)S(1)} %bitcast.49, s32[1024]{0:T(1024)S(1)} %pad_clamp_fusion.1), kind=kCustom, calls=%fused_computation.1.clone | custom fusion | bytes 8388864 | tf_op jit(solution)/shard_map/jit(_take)/gather | solution.py:65
  133.9 2.8 %gather_fusion.2 = bf16[64,128,256]{2,1,0:T(8,128)(2,1)} fusion(bf16[4,128,256]{2,1,0:T(8,128)(2,1)S(1)} %bitcast.48, s32[1024]{0:T(1024)S(1)} %pad_clamp_fusion.1), kind=kCustom, calls=%fused_computation.clone | custom fusion | bytes 8388864 | tf_op jit(solution)/shard_map/jit(_take)/gather | solution.py:64
  136.7 5.9 %broadcast_select_fusion.1 = (bf16[64,128,256]{2,1,0:T(8,128)(2,1)}, bf16[64,128,256]{2,1,0:T(8,128)(2,1)}) fusion(bf16[64,128,256]{2,1,0:T(8,128)(2,1)} %gather_fusion.2, pred[64]{0:T(512)(128)(4,1)S(1)} %compare_and_fusion.1, bf16[64,128,256]{2,1,0:T(8,128)(2,1)} %gather_fusion.3), kind=kLoop, calls=%fused_computation.5 | loop fusion | flops 4194304 | bytes 16777280 | tf_op jit(solution)/shard_map/jit(_take)/select_n | solution.py:64
  142.5 30.9 %all-to-all-done = bf16[64,1,64,256]{3,2,1,0:T(8,128)(2,1)} async-done(((bf16[64,1,64,256]{3,2,1,0:T(8,128)(2,1)}), bf16[64,1,64,256]{3,2,1,0:T(8,128)(2,1)}, u32[]{:S(2)}, u32[]{:S(2)}) %all-to-all-start) | async-done | bytes 2097184 | tf_op jit(solution)/shard_map/all_to_all | solution.py:60
  173.5 3.7 %exponential_reduce_fusion = (f32[64,64]{1,0:T(8,128)S(1)}, f32[64,64,128]{2,1,0:T(8,128)S(1)}) fusion(bf16[64,128,256]{2,1,0:T(8,128)(2,1)} %get-tuple-element.10, bf16[64,64,256]{2,1,0:T(8,128)(2,1)} %bitcast.3), kind=kOutput, calls=%fused_computation.17 | convolution fusion | flops 134737920 | bytes 5259264 | tf_op jit(solution)/shard_map/sqd,skd->sqk/dot_general | solution.py:72
  177.2 3.1 %exponential_reduce_fusion.1 = (f32[64,64]{1,0:T(8,128)S(1)}, f32[64,64,128]{2,1,0:T(8,128)S(1)}) fusion(bf16[64,128,256]{2,1,0:T(8,128)(2,1)S(1)} %copy-done.1, bf16[64,64,256]{2,1,0:T(8,128)(2,1)} %bitcast.3), kind=kOutput, calls=%fused_computation.18 | convolution fusion | flops 134737920 | bytes 5259264 | tf_op jit(solution)/shard_map/sqd,skd->sqk/dot_general | solution.py:72
  181.3 1.8 fusion.11
  183.8 7.0 %all-to-all-start.2 = ((bf16[64,1,128]{2,1,0:T(2,128)(2,1)}), bf16[64,1,128]{2,1,0:T(2,128)(2,1)S(1)}, u32[]{:S(2)}, u32[]{:S(2)}) async-start(bf16[64,1,128]{2,1,0:T(2,128)(2,1)} %copy.56), calls=%async_computation.2 | async-start | bytes 65536 | tf_op jit(solution)/shard_map/all_to_all | solution.py:93
  190.8 2.8 %maximum_bitcast_fusion = bf16[64,1,64,256]{3,2,1,0:T(8,128)(2,1)} fusion(bf16[64,64,128]{2,1,0:T(8,128)(2,1)} %fusion.11, bf16[64,64,128]{2,1,0:T(8,128)(2,1)S(1)} %fusion.8), kind=kLoop, calls=%fused_computation.14 | loop fusion | flops 4194304 | bytes 4194304 | tf_op jit(solution)/shard_map/reshape | solution.py:90
  193.7 6.5 %all-to-all-done.2 = bf16[64,1,128]{2,1,0:T(2,128)(2,1)S(1)} async-done(((bf16[64,1,128]{2,1,0:T(2,128)(2,1)}), bf16[64,1,128]{2,1,0:T(2,128)(2,1)S(1)}, u32[]{:S(2)}, u32[]{:S(2)}) %all-to-all-start.2) | async-done | bytes 16416 | tf_op jit(solution)/shard_map/all_to_all | solution.py:93
  200.1 5.6 %all-to-all-start.3 = ((bf16[64,1,64,256]{3,2,1,0:T(8,128)(2,1)}), bf16[64,1,64,256]{3,2,1,0:T(8,128)(2,1)}, u32[]{:S(2)}, u32[]{:S(2)}) async-start(bf16[64,1,64,256]{3,2,1,0:T(8,128)(2,1)} %maximum_bitcast_fusion), calls=%async_computation.3 | async-start | bytes 4194304 | tf_op jit(solution)/shard_map/all_to_all | solution.py:92
  206.9 48.4 %all-to-all-done.3 = bf16[64,1,64,256]{3,2,1,0:T(8,128)(2,1)} async-done(((bf16[64,1,64,256]{3,2,1,0:T(8,128)(2,1)}), bf16[64,1,64,256]{3,2,1,0:T(8,128)(2,1)}, u32[]{:S(2)}, u32[]{:S(2)}) %all-to-all-start.3) | async-done | bytes 2097184 | tf_op jit(solution)/shard_map/all_to_all | solution.py:92
  255.3 4.2 %copy.61 = bf16[8,8,64,256]{3,1,2,0:T(8,128)(2,1)} copy(bf16[8,8,64,256]{3,2,1,0:T(8,128)(2,1)} %bitcast.24) | data formatting | bytes 4194304
  259.5 3.6 %gather_fusion.1 = bf16[24,16384]{1,0:T(8,128)(2,1)S(1)} fusion(bf16[64,16384]{1,0:T(8,128)(2,1)} %bitcast.50, s32[1024]{0:T(1024)S(1)} %pad_clamp_fusion), kind=kCustom, calls=%fused_computation.3 | custom fusion | bytes 1572960 | tf_op jit(solution)/shard_map/jit(_take)/gather | solution.py:96
  (50 shorter events, 9.3 us)
Async XLA Ops:
  6.5 95.7 %copy-start = (bf16[4096,256]{1,0:T(8,128)(2,1)S(1)}, bf16[4096,256]{1,0:T(8,128)(2,1)}, u32[]{:S(2)}) copy-start(bf16[4096,256]{1,0:T(8,128)(2,1)} %param.11) | copy-start | bytes 6291460
  6.5 3.5 %copy-start.3 = (s32[12,2]{0,1:T(2,128)S(1)}, s32[12,2]{0,1:T(2,128)}, u32[]{:S(2)}) copy-start(s32[12,2]{0,1:T(2,128)} %param.15) | copy-start | bytes 292
  6.5 95.7 %all-gather.2.cloned.1.call-start = ((), (), s32[]{:S(2)}) async-start(), calls=%async_computation.4 | async-start | bytes 6815744 | tf_op jit(solution)/shard_map/all_gather | solution.py:26
  11.2 102.1 %all-to-all-start.1 = ((s32[64,1,1]{2,1,0:T(1,128)}), s32[64,1,1]{2,1,0:T(1,128)S(1)}, u32[]{:S(2)}, u32[]{:S(2)}) async-start(s32[64,1,1]{2,1,0:T(1,128)} %copy.55), calls=%async_computation.1 | async-start | bytes 65536 | tf_op jit(solution)/shard_map/all_to_all | solution.py:61
  113.3 60.2 %all-to-all-start = ((bf16[64,1,64,256]{3,2,1,0:T(8,128)(2,1)}), bf16[64,1,64,256]{3,2,1,0:T(8,128)(2,1)}, u32[]{:S(2)}, u32[]{:S(2)}) async-start(bf16[64,1,64,256]{3,2,1,0:T(8,128)(2,1)} %copy.54), calls=%async_computation | async-start | bytes 4194304 | tf_op jit(solution)/shard_map/all_to_all | solution.py:60
  123.9 4.3 %copy-start.4 = (bf16[4,128,4096]{2,1,0:T(8,128)(2,1)S(1)}, bf16[4,128,4096]{2,1,0:T(8,128)(2,1)}, u32[]{:S(2)}) copy-start(bf16[4,128,4096]{2,1,0:T(8,128)(2,1)} %param.14) | copy-start | bytes 12582916
  123.9 4.7 %copy-start.5 = (bf16[4096,256]{1,0:T(8,128)(2,1)S(1)}, bf16[4096,256]{1,0:T(8,128)(2,1)}, u32[]{:S(2)}) copy-start(bf16[4096,256]{1,0:T(8,128)(2,1)} %param.13) | copy-start | bytes 6291460
  173.5 3.7 %copy-start.1 = (bf16[64,128,256]{2,1,0:T(8,128)(2,1)S(1)}, bf16[64,128,256]{2,1,0:T(8,128)(2,1)}, u32[]{:S(2)}) copy-start(bf16[64,128,256]{2,1,0:T(8,128)(2,1)} %get-tuple-element.10) | copy-start | bytes 12582916
  177.2 3.1 %copy-start.2 = (bf16[64,128,256]{2,1,0:T(8,128)(2,1)S(1)}, bf16[64,128,256]{2,1,0:T(8,128)(2,1)}, u32[]{:S(2)}) copy-start(bf16[64,128,256]{2,1,0:T(8,128)(2,1)} %get-tuple-element.11) | copy-start | bytes 12582916
  183.8 16.3 %all-to-all-start.2 = ((bf16[64,1,128]{2,1,0:T(2,128)(2,1)}), bf16[64,1,128]{2,1,0:T(2,128)(2,1)S(1)}, u32[]{:S(2)}, u32[]{:S(2)}) async-start(bf16[64,1,128]{2,1,0:T(2,128)(2,1)} %copy.56), calls=%async_computation.2 | async-start | bytes 65536 | tf_op jit(solution)/shard_map/all_to_all | solution.py:93
  200.1 55.2 %all-to-all-start.3 = ((bf16[64,1,64,256]{3,2,1,0:T(8,128)(2,1)}), bf16[64,1,64,256]{3,2,1,0:T(8,128)(2,1)}, u32[]{:S(2)}, u32[]{:S(2)}) async-start(bf16[64,1,64,256]{3,2,1,0:T(8,128)(2,1)} %maximum_bitcast_fusion), calls=%async_computation.3 | async-start | bytes 4194304 | tf_op jit(solution)/shard_map/all_to_all | solution.py:92
Sparse Core Ops, SparseCore 0:
  10.2 92.0 all-gather.1
where the time goes:
time: 273 us; the launch traced here: 272 us
  waiting for transfers between devices  162 us (59%)
  starting transfers between devices  37.8 us (14%)
  matrix products  21.5 us (8%)
  local copies, waits for them, and re-layouts  20.8 us (8%)
  other arithmetic  15.5 us (6%)
  between operations  13.7 us (5%)
    all_gather x1, waiting for transfers between devices, per_device(): lax.all_gather((stream * factor * norm_gain).astype(jnp.bfloat16), 'mp',...  76.4 us
    all_to_all x1, waiting for transfers between devices, per_device(): lax.all_to_all(result, 'db', split_axis=0, concat_axis=0, tiled=True)  48.4 us
    all_to_all x1, waiting for transfers between devices, per_device(): lax.all_to_all(send_queries, 'db', split_axis=0, concat_axis=0, tiled=True)  30.9 us
    all_to_all x1, starting transfers between devices, per_device(): lax.all_to_all(send_rows, 'db', split_axis=0, concat_axis=0, tiled=True)  14.5 us
    all_to_all x1, starting transfers between devices, per_device(): lax.all_to_all(send_queries, 'db', split_axis=0, concat_axis=0, tiled=True)  10.6 us
    all_to_all x1, starting transfers between devices, per_device(): lax.all_to_all(lse_rows.astype(jnp.bfloat16), 'db', split_axis=0, concat_...  7.02 us
    dot_general x2, matrix products, per_device(): jnp.einsum('sqd,skd->sqk', asking[:, :, serve_first_col:serve_last_col],...  6.76 us
    all_to_all x1, waiting for transfers between devices, per_device(): lax.all_to_all(lse_rows.astype(jnp.bfloat16), 'db', split_axis=0, concat_...  6.45 us
  transfers between devices with their start and end apart: 5, of which 4 were waited for; matrix products, arithmetic and copies ran while one was open for 13% of the time, Pallas kernels for 0%

commit v1 on v0

v1 whole, which is shorter than its diff:
```python
import jax
import jax.numpy as jnp
from jax import lax
from jax.experimental import pallas as pl
from jax.experimental.pallas import tpu as pltpu
from jax.sharding import PartitionSpec as P

HD = 128
BLOCK = 64
NBR = 128
EPS = 1e-6
NX, NY, NZ = 4, 8, 12
D = 4096
ROWS = 4
NEG = -1e30
RR = 80
MESH = pl.DeviceIdType.MESH
BF = jnp.bfloat16
F32 = jnp.float32


def kernel(
    hidden, gain, wq, wk, wv, bank, ids, out,
    hid_v, wq_v, wk_v, wv_v, bank_v, zb, kv, kvs, qs, q_in, r_out, r_in, ids_v, ids_s,
    lsem, z_ss, z_rs, y_ss, y_rs, x_ss, x_rs, b_ss, b_rs, q_ss, q_rs, r_ss, r_rs, i_ss, i_rs,
):
    db = lax.axis_index("db")
    z = lax.axis_index("mp")
    c = db % 2
    x = (db // 2) % NX
    y = db // (2 * NX)
    x0 = x % 2
    x1 = x // 2

    def dev(yy, xx, cc, zz):
        return {"db": (yy * NX + xx) * 2 + cc, "mp": zz}

    xs = (x, x + 1 - 2 * x0, (x + 2) % NX, NX - 1 - x)
    z_dev = (dev(y, x, c, (z + 1) % NZ), dev(y, x, c, (z + NZ - 1) % NZ))
    y_dev = (dev((y + 1) % NY, x, c, z), dev((y + NY - 1) % NY, x, c, z))
    x_dev = tuple(dev(y, xx, c, z) for xx in xs)
    sib = dev(y, x, 1 - c, z)
    peers = z_dev + y_dev + x_dev[1:] + (sib,)

    loads = [
        pltpu.make_async_copy(a, b, lsem.at[n])
        for n, (a, b) in enumerate(
            ((hidden, hid_v), (bank, bank_v), (wk, wk_v), (wv, wv_v), (wq, wq_v), (ids, ids_v.at[0]))
        )
    ]
    for load in loads:
        load.start()
    barrier = pltpu.get_barrier_semaphore()
    for peer in peers:
        pl.semaphore_signal(barrier, inc=1, device_id=peer, device_id_type=MESH)

    def copy(src, dst, ss, rs, to):
        return pltpu.make_async_remote_copy(
            src_ref=src, dst_ref=dst, send_sem=ss, recv_sem=rs, device_id=to, device_id_type=MESH
        )

    sent = []

    def send(src, dst, ss, rs, to):
        one = copy(src, dst, ss, rs, to)
        one.start()
        sent.append(one)

    def landed(dst, ss, rs):
        copy(dst, dst, ss, rs, sib).wait_recv()

    loads[0].wait()

    def norm_rows(n, carry):
        rows = pl.ds(pl.multiple_of(n * 16, 16), 16)
        stream = hid_v[rows, :].astype(F32)
        factor = lax.rsqrt(jnp.mean(stream * stream, axis=-1, keepdims=True) + EPS)
        zb[0, rows, :] = (stream * factor * gain[...]).astype(BF)
        return carry

    lax.fori_loop(0, BLOCK // 16, norm_rows, 0)
    pl.semaphore_wait(barrier, len(peers))

    def z_part(slot, sub):
        return zb.at[slot, pl.ds(sub * 32, 32), :]

    def z_slot(way, s):
        return 0 if s == 0 else (11 if s == 6 else 2 * s - 1 + way)

    def z_send(way, s, sub):
        send(
            z_part(z_slot(way, s), sub), z_part(z_slot(way, s + 1), sub),
            z_ss.at[way, s, sub], z_rs.at[way, s, sub], z_dev[way],
        )

    def z_wait(way, s, sub):
        landed(z_part(z_slot(way, s), sub), z_ss.at[way, s - 1, sub], z_rs.at[way, s - 1, sub])

    def z_needed(way, s, sub):
        return s < 6 or sub == way

    for sub in range(2):
        for way in range(2):
            z_send(way, 0, sub)

    loads[5].wait()
    for j in (1, 2, 3):
        send(ids_v.at[0], ids_v.at[j], i_ss.at[j], i_rs.at[j], x_dev[j])

    def unit(yy, cc, bit):
        return ((yy * 2 + cc) * 2 + bit) * ROWS

    own = unit(y, c, x0)
    loads[1].wait()
    for which in range(2):
        loads[2 + which].wait()
        weight = (wk_v, wv_v)[which]

        def project(n, carry):
            got = jnp.dot(
                bank_v[pl.ds(n * 2, 2)].reshape(2 * NBR, D), weight[...], preferred_element_type=F32
            )
            low, high = got[:, :HD], got[:, HD:]
            mine = jnp.where(x0 == 0, low, high).astype(BF)
            other = jnp.where(x0 == 0, high, low).astype(BF)
            for a in range(2):
                kv[own + n * 2 + a, which] = mine[a * NBR : (a + 1) * NBR]
                kvs[n * 2 + a, which] = other[a * NBR : (a + 1) * NBR]
            return carry

        lax.fori_loop(0, ROWS // 2, project, 0)

    def y_at(way, s):
        return (y + NY - s) % NY if way == 0 else (y + s) % NY

    def kv_part(yy, cc, sub):
        return kv.at[pl.ds(unit(yy, cc, x0 if sub == 0 else 1 - x0), ROWS)]

    def y_send(way, s, sub):
        part = kv_part(y_at(way, s), c, sub)
        send(part, part, y_ss.at[way, s, sub], y_rs.at[way, s, sub], y_dev[way])

    def y_wait(way, s, sub):
        part = kv_part(y_at(way, s), c, sub)
        landed(part, y_ss.at[way, s - 1, sub], y_rs.at[way, s - 1, sub])

    def b_slot(way, s):
        return 0 if s == 0 else (7 if s == 4 else 2 * s - 1 + way)

    def b_send(way, s, sub):
        part = kv_part(y_at(way, s), c, sub)
        n = b_slot(way, s)
        send(part, part, b_ss.at[n, sub], b_rs.at[n, sub], sib)

    def b_wait(way, s, sub):
        n = b_slot(way, s)
        landed(kv_part(y_at(way, s), 1 - c, sub), b_ss.at[n, sub], b_rs.at[n, sub])

    send(kvs, kv.at[pl.ds(own, ROWS)], x_ss.at[0], x_rs.at[0], x_dev[1])
    for way in range(2):
        y_send(way, 0, 0)
    b_send(0, 0, 0)

    def y_needed(way, s, sub):
        return s < 4 or sub == way

    def y_step(s, sub):
        if s == 0:
            if sub == 1:
                landed(kv_part(y, c, 1), x_ss.at[0], x_rs.at[0])
                for way in range(2):
                    y_send(way, 0, 1)
                b_send(0, 0, 1)
            return
        for way in range(2):
            if y_needed(way, s, sub):
                y_wait(way, s, sub)
                if s < 4 and y_needed(way, s + 1, sub):
                    y_send(way, s, sub)
                b_send(way, s, sub)

    scale = HD ** (-0.5)

    def slots(g):
        return (0, 1) if g == 0 else ((11, 1) if g == 6 else (2 * g - 1, 2))

    def q_part(ref, g):
        first, count = slots(g)
        return ref.at[pl.ds(first, count)]

    def queries(g):
        first, count = slots(g)
        got = jnp.dot(
            zb[first : first + count].reshape(count * BLOCK, D), wq_v[...],
            preferred_element_type=F32,
        ) * scale
        low, high = got[:, :HD], got[:, HD:]
        mine = jnp.where(x0 == 0, low, high).astype(BF)
        other = jnp.where(x0 == 0, high, low).astype(BF)
        for a in range(count):
            q_in[0, first + a] = mine[a * BLOCK : (a + 1) * BLOCK]
            qs[first + a] = other[a * BLOCK : (a + 1) * BLOCK]
        for j in (2, 1, 3):
            src = q_part(q_in.at[0], g) if j == 2 else q_part(qs, g)
            send(src, q_part(q_in.at[j], g), q_ss.at[j, g], q_rs.at[j, g], x_dev[j])

    def block_of(slot):
        s = (slot + 1) // 2
        sign = 1 - 2 * (slot % 2)
        return (z + NZ + sign * s) % NZ

    diag = lax.broadcasted_iota(jnp.int32, (BLOCK, HD), 0) == lax.broadcasted_iota(
        jnp.int32, (BLOCK, HD), 1
    )
    row_no = lax.broadcasted_iota(jnp.int32, (16, HD), 0)

    def attend(j, slot):
        block = block_of(slot)
        q = q_in[j, slot]
        scores, rows = [], []
        for k in range(2):
            nbr = ids_s[j, block, k]
            shard = nbr // ROWS
            col = (shard // 2) % NX
            row = ((shard // (2 * NX) * 2 + shard % 2) * 2 + col % 2) * ROWS + nbr % ROWS
            s = lax.dot_general(q, kv[row, 0], (((1,), (1,)), ((), ())), preferred_element_type=F32)
            scores.append(jnp.where(col // 2 == x1, s, NEG))
            rows.append(row)
        top = jnp.max(jnp.maximum(scores[0], scores[1]), axis=-1, keepdims=True)
        e0 = jnp.exp(scores[0] - top)
        e1 = jnp.exp(scores[1] - top)
        denom = jnp.sum(e0 + e1, axis=-1, keepdims=True)
        o = jnp.dot(e0.astype(BF), kv[rows[0], 1], preferred_element_type=F32) + jnp.dot(
            e1.astype(BF), kv[rows[1], 1], preferred_element_type=F32
        )
        r_out[j, slot, 0:BLOCK, :] = (o / denom).astype(BF)
        lse = jnp.sum(jnp.where(diag, top + jnp.log(denom), 0.0), axis=0, keepdims=True)
        hi = lse.astype(BF).astype(F32)
        mid = (lse - hi).astype(BF).astype(F32)
        lo = lse - hi - mid
        packed = jnp.where(row_no == 0, hi, jnp.where(row_no == 1, mid, jnp.where(row_no == 2, lo, 0.0)))
        r_out[j, slot, BLOCK:RR, :] = packed.astype(BF)

    def r_copy(j, g, first, count):
        return copy(
            r_out.at[j, pl.ds(first, count)], r_in.at[j, pl.ds(first, count)],
            r_ss.at[j, g], r_rs.at[j, g], x_dev[j],
        )

    def serve(g, first, count):
        for j in (1, 2, 3):
            landed(q_in.at[j, pl.ds(first, count)], q_ss.at[j, g], q_rs.at[j, g])

        def one(j, carry):
            for a in range(count):
                attend(j, first + a)
            return carry

        lax.fori_loop(0, NX, one, 0)
        for j in (1, 2, 3):
            r_copy(j, g, first, count).start()

    def lse_of(ref, j, slot):
        tile = ref[j, slot, BLOCK:RR, :].astype(F32)
        return jnp.sum(tile, axis=0, keepdims=True)

    def column(row):
        return jnp.sum(jnp.where(diag, row, 0.0), axis=-1, keepdims=True)

    def merge(g, first, count):
        for j in (1, 2, 3):
            landed(r_in.at[j, pl.ds(first, count)], r_ss.at[j, g], r_rs.at[j, g])
        for a in range(count):
            slot = first + a
            rows = pl.ds(pl.multiple_of(block_of(slot) * BLOCK, BLOCK), BLOCK)
            for head, (ra, ja), (rb, jb) in (
                (x0, (r_out, 0), (r_in, 2)),
                (1 - x0, (r_in, 1), (r_in, 3)),
            ):
                gap = lse_of(rb, jb, slot) - lse_of(ra, ja, slot)
                wa = column(1.0 / (1.0 + jnp.exp(gap)))
                wb = column(1.0 / (1.0 + jnp.exp(-gap)))
                both = wa * ra[ja, slot, 0:BLOCK, :].astype(F32) + wb * rb[
                    jb, slot, 0:BLOCK, :
                ].astype(F32)
                out[rows, pl.ds(pl.multiple_of(head * HD, HD), HD)] = both.astype(BF)

    loads[4].wait()
    queries(0)
    for s in range(1, 7):
        for sub in range(2):
            for way in range(2):
                if z_needed(way, s, sub):
                    z_wait(way, s, sub)
                    if s < 6 and z_needed(way, s + 1, sub):
                        z_send(way, s, sub)
            if s <= 5:
                y_step(s - 1, sub)
        queries(s)
        if s == 5:
            for j in (1, 2, 3):
                landed(ids_v.at[j], i_ss.at[j], i_rs.at[j])
            to_smem = pltpu.make_async_copy(ids_v, ids_s, lsem.at[6])
            to_smem.start()
            to_smem.wait()
            for t in range(5):
                for way in range(2):
                    for sub in range(2):
                        if (way == 0 or t > 0) and y_needed(way, t, sub):
                            b_wait(way, t, sub)
            serve(0, 0, 1)

            def serve_pair(g, carry):
                serve(g, 2 * g - 1, 2)
                return carry

            lax.fori_loop(1, 5, serve_pair, 0)
    serve(5, 9, 2)
    serve(6, 11, 1)
    merge(0, 0, 1)

    def merge_pair(g, carry):
        merge(g, 2 * g - 1, 2)
        return carry

    lax.fori_loop(1, 6, merge_pair, 0)
    merge(6, 11, 1)

    for one in sent:
        one.wait_send()
    for j in (1, 2, 3):
        r_copy(j, 0, 0, 1).wait_send()
        r_copy(j, 6, 11, 1).wait_send()

        def pair_sent(g, carry):
            r_copy(j, g, 2 * g - 1, 2).wait_send()
            return carry

        lax.fori_loop(1, 6, pair_sent, 0)


def per_device(hidden, norm_gain, query_weight, key_weight, value_weight, bank, neighbour_ids):
    hbm = pl.BlockSpec(memory_space=pl.ANY)
    vmem = pl.BlockSpec(memory_space=pltpu.VMEM)
    dma = pltpu.SemaphoreType.DMA
    width = query_weight.shape[1]
    return pl.pallas_call(
        kernel,
        out_shape=jax.ShapeDtypeStruct((NZ * BLOCK, width), BF),
        in_specs=[hbm, vmem, hbm, hbm, hbm, hbm, hbm],
        out_specs=vmem,
        scratch_shapes=[
            pltpu.VMEM((BLOCK, D), BF),
            pltpu.VMEM((D, width), BF),
            pltpu.VMEM((D, width), BF),
            pltpu.VMEM((D, width), BF),
            pltpu.VMEM((ROWS, NBR, D), BF),
            pltpu.VMEM((NZ, BLOCK, D), BF),
            pltpu.VMEM((NY * 2 * 2 * ROWS, 2, NBR, HD), BF),
            pltpu.VMEM((ROWS, 2, NBR, HD), BF),
            pltpu.VMEM((NZ, BLOCK, HD), BF),
            pltpu.VMEM((NX, NZ, BLOCK, HD), BF),
            pltpu.VMEM((NX, NZ, RR, HD), BF),
            pltpu.VMEM((NX, NZ, RR, HD), BF),
            pltpu.VMEM((NX, NZ, 2), jnp.int32),
            pltpu.SMEM((NX, NZ, 2), jnp.int32),
            dma((7,)),
            dma((2, 6, 2)),
            dma((2, 6, 2)),
            dma((2, 4, 2)),
            dma((2, 4, 2)),
            dma((1,)),
            dma((1,)),
            dma((8, 2)),
            dma((8, 2)),
            dma((4, 7)),
            dma((4, 7)),
            dma((4, 7)),
            dma((4, 7)),
            dma((4,)),
            dma((4,)),
        ],
        compiler_params=pltpu.CompilerParams(
            collective_id=0, has_side_effects=True, vmem_limit_bytes=56 * 1024 * 1024
        ),
    )(
        hidden, norm_gain.reshape(1, D), query_weight, key_weight, value_weight, bank, neighbour_ids
    )


def solution(mesh):
    placed = (
        P(("db", "mp"), None),
        P(),
        P(None, "mp"),
        P(None, "mp"),
        P(None, "mp"),
        P("db", None, None),
        P("db", None),
    )
    return jax.shard_map(
        per_device, mesh=mesh, in_specs=placed, out_specs=P("db", "mp"), check_vma=False
    )
```

time: 273 us -> 107 us (0.39)
  waiting for transfers between devices: 162 us -> 0 us
  Pallas kernels: 0 us -> 103 us
  starting transfers between devices: 37.8 us -> 0 us
  matrix products: 21.5 us -> 0 us
  local copies, waits for them, and re-layouts: 20.8 us -> 3.13 us
  other arithmetic: 15.5 us -> 0 us
  between operations: 13.7 us -> 0.01 us
    pallas_call x0 -> x1, Pallas kernels: none -> 103 us  [per_device(): pl.pallas_call(kernel, out_shape=jax.ShapeDtypeStruct((NZ * BLOCK, width)...]
    all_to_all x4 -> x0, waiting for transfers between devices: 85.8 us -> none  [the longest x1 48.4 us: per_device(): lax.all_to_all(result, 'db', split_axis=0, concat_axis=0, tiled=True)]
    all_gather x1 -> x0, waiting for transfers between devices: 76.4 us -> none  [per_device(): lax.all_gather((stream * factor * norm_gain).astype(jnp.bfloat16), 'mp',...]
    all_to_all x4 -> x0, starting transfers between devices: 37.8 us -> none  [the longest x1 14.5 us: per_device(): lax.all_to_all(send_rows, 'db', split_axis=0, concat_axis=0, tiled=True)]
    dot_general x8 -> x0, matrix products: 21.5 us -> none  [the longest x2 6.76 us: per_device(): jnp.einsum('sqd,skd->sqk', asking[:, :, serve_first_col:serve_last_col],...]
    gather x5 -> x0, local copies, waits for them, and re-layouts: 9.76 us -> none  [the longest x1 3.58 us: per_device(): jnp.take(back_result.reshape(slot_count, BLOCK * local_width), target, ax...]
    select_n x5 -> x0, other arithmetic: 6.03 us -> none  [the longest x2 5.86 us: per_device(): near_keys = jnp.take(bank_keys, flat_rows, axis=0)]
    reshape x2 -> x0, other arithmetic: 2.85 us -> none  [the longest x1 2.85 us: per_device(): jnp.concatenate(results, axis=-1)]
  transfers between devices with their start and end apart: 5 -> 0, of which waited for: 4 -> 0; matrix products, arithmetic and copies ran while one was open for 13% -> 0% of each run, Pallas kernels for 0% -> 0%
where the time goes in v1:
time: 107 us; the launch traced here: 106 us
  Pallas kernels  103 us (96%)
  local copies, waits for them, and re-layouts  3.13 us (3%)
    pallas_call x1, Pallas kernels, per_device(): pl.pallas_call(kernel, out_shape=jax.ShapeDtypeStruct((NZ * BLOCK, width)...  103 us
    unnamed x2, local copies, waits for them, and re-layouts  3.13 us

profile of v1, /device:TPU:1, one launch (start us, length us, event | category | flops | bytes accessed | tf_op | source)
XLA Modules:
  0.0 106.4 jit_solution(14708726678131876231)
XLA Ops:
  0.0 1.4 %copy.8.ids = s32[12,2]{1,0:T(8,128)} copy(s32[12,2]{0,1:T(2,128)} %param.13) | data formatting | bytes 192 | tf_op args[6]
  1.4 103.3 %shard_map.73 = bf16[768,256]{1,0:T(8,128)(2,1)} custom-call(bf16[64,4096]{1,0:T(8,128)(2,1)} %hidden.1, f32[1,4096]{1,0:T(1,128)} %bitcast.1, bf16[4096,256]{1,0:T(8,128)(2,1)} %wq.1, bf16[4096,256]{1,0:T(8,128)(2,1)} %wk.1, bf16[4096,256]{1,0:T(8,128)(2,1)} %wv.1, bf16[4,128,4096]{2,1,0:T(8,128)(2,1)} %bank.1, s32[12,2]{1,0:T(8,128)} %copy.8.ids), custom_call_target="tpu_custom_call" | custom-call | tf_op jit(solution)/shard_map/pallas_call | solution.py:347
  104.6 1.8 %copy.10 = bf16[768,256]{1,0:T(8,128)(2,1)} copy(bf16[768,256]{1,0:T(8,128)(2,1)} %shard_map.73) | data formatting | bytes 786432

commit v2 on v1

--- a/solution.py
+++ b/solution.py
@@ -214,32 +214,50 @@
     )
     row_no = lax.broadcasted_iota(jnp.int32, (16, HD), 0)
 
-    def attend(j, slot):
-        block = block_of(slot)
-        q = q_in[j, slot]
-        scores, rows = [], []
-        for k in range(2):
-            nbr = ids_s[j, block, k]
-            shard = nbr // ROWS
-            col = (shard // 2) % NX
-            row = ((shard // (2 * NX) * 2 + shard % 2) * 2 + col % 2) * ROWS + nbr % ROWS
-            s = lax.dot_general(q, kv[row, 0], (((1,), (1,)), ((), ())), preferred_element_type=F32)
-            scores.append(jnp.where(col // 2 == x1, s, NEG))
-            rows.append(row)
-        top = jnp.max(jnp.maximum(scores[0], scores[1]), axis=-1, keepdims=True)
-        e0 = jnp.exp(scores[0] - top)
-        e1 = jnp.exp(scores[1] - top)
-        denom = jnp.sum(e0 + e1, axis=-1, keepdims=True)
-        o = jnp.dot(e0.astype(BF), kv[rows[0], 1], preferred_element_type=F32) + jnp.dot(
-            e1.astype(BF), kv[rows[1], 1], preferred_element_type=F32
-        )
-        r_out[j, slot, 0:BLOCK, :] = (o / denom).astype(BF)
-        lse = jnp.sum(jnp.where(diag, top + jnp.log(denom), 0.0), axis=0, keepdims=True)
-        hi = lse.astype(BF).astype(F32)
-        mid = (lse - hi).astype(BF).astype(F32)
-        lo = lse - hi - mid
-        packed = jnp.where(row_no == 0, hi, jnp.where(row_no == 1, mid, jnp.where(row_no == 2, lo, 0.0)))
-        r_out[j, slot, BLOCK:RR, :] = packed.astype(BF)
+    lane = lax.broadcasted_iota(jnp.int32, (1, 2 * NBR), 1)
+
+    def attend(items):
+        loaded = []
+        for j, slot in items:
+            block = block_of(slot)
+            rows, bias = [], []
+            for k in range(2):
+                nbr = ids_s[j, k, block]
+                shard = nbr // ROWS
+                col = (shard // 2) % NX
+                rows.append(
+                    ((shard // (2 * NX) * 2 + shard % 2) * 2 + col % 2) * ROWS + nbr % ROWS
+                )
+                bias.append(jnp.where(col // 2 == x1, 0.0, NEG))
+            loaded.append((
+                q_in[j, slot],
+                jnp.concatenate([kv[rows[0], 0], kv[rows[1], 0]], axis=0),
+                jnp.concatenate([kv[rows[0], 1], kv[rows[1], 1]], axis=0),
+                jnp.where(lane < NBR, bias[0], bias[1]),
+            ))
+        scores = [
+            lax.dot_general(q, keys, (((1,), (1,)), ((), ())), preferred_element_type=F32) + bias
+            for q, keys, _, bias in loaded
+        ]
+        expo = [jnp.exp(s) for s in scores]
+        denom = [jnp.sum(e, axis=-1, keepdims=True) for e in expo]
+        down = [jnp.where(d > 1.0, 0.0625, 1.0) for d in denom]
+        inverse = [jnp.where(d > 0.0, 1.0 / (d * w), 0.0) for d, w in zip(denom, down)]
+        probs = [(e * w * v).astype(BF) for e, w, v in zip(expo, down, inverse)]
+        parts = [
+            jnp.dot(p, values, preferred_element_type=F32)
+            for p, (_, _, values, _) in zip(probs, loaded)
+        ]
+        for (j, slot), part, d in zip(items, parts, denom):
+            r_out[j, slot, 0:BLOCK, :] = part.astype(BF)
+            total = jnp.sum(jnp.where(diag, d, 0.0), axis=0, keepdims=True)
+            hi = total.astype(BF).astype(F32)
+            mid = (total - hi).astype(BF).astype(F32)
+            lo = total - hi - mid
+            packed = jnp.where(
+                row_no == 0, hi, jnp.where(row_no == 1, mid, jnp.where(row_no == 2, lo, 0.0))
+            )
+            r_out[j, slot, BLOCK:RR, :] = packed.astype(BF)
 
     def r_copy(j, g, first, count):
         return copy(
@@ -251,18 +269,12 @@
         for j in (1, 2, 3):
             landed(q_in.at[j, pl.ds(first, count)], q_ss.at[j, g], q_rs.at[j, g])
 
-        def one(j, carry):
-            for a in range(count):
-                attend(j, first + a)
-            return carry
-
-        lax.fori_loop(0, NX, one, 0)
+        attend([(j, first + a) for j in (1, 2, 3, 0) for a in range(count)])
         for j in (1, 2, 3):
             r_copy(j, g, first, count).start()
 
-    def lse_of(ref, j, slot):
-        tile = ref[j, slot, BLOCK:RR, :].astype(F32)
-        return jnp.sum(tile, axis=0, keepdims=True)
+    def sum_of(ref, j, slot):
+        return jnp.sum(ref[j, slot, BLOCK:RR, :].astype(F32), axis=0, keepdims=True)
 
     def column(row):
         return jnp.sum(jnp.where(diag, row, 0.0), axis=-1, keepdims=True)
@@ -277,13 +289,13 @@
                 (x0, (r_out, 0), (r_in, 2)),
                 (1 - x0, (r_in, 1), (r_in, 3)),
             ):
-                gap = lse_of(rb, jb, slot) - lse_of(ra, ja, slot)
-                wa = column(1.0 / (1.0 + jnp.exp(gap)))
-                wb = column(1.0 / (1.0 + jnp.exp(-gap)))
-                both = wa * ra[ja, slot, 0:BLOCK, :].astype(F32) + wb * rb[
+                la, lb = sum_of(ra, ja, slot), sum_of(rb, jb, slot)
+                both = jnp.where(la + lb > 0.0, la + lb, 1.0)
+                wa, wb = column(la / both), column(lb / both)
+                mixed = wa * ra[ja, slot, 0:BLOCK, :].astype(F32) + wb * rb[
                     jb, slot, 0:BLOCK, :
                 ].astype(F32)
-                out[rows, pl.ds(pl.multiple_of(head * HD, HD), HD)] = both.astype(BF)
+                out[rows, pl.ds(pl.multiple_of(head * HD, HD), HD)] = mixed.astype(BF)
 
     loads[4].wait()
     queries(0)
@@ -294,15 +306,17 @@
                     z_wait(way, s, sub)
                     if s < 6 and z_needed(way, s + 1, sub):
                         z_send(way, s, sub)
-            if s <= 5:
+            if s <= 4:
                 y_step(s - 1, sub)
         queries(s)
-        if s == 5:
+        if s == 4:
             for j in (1, 2, 3):
                 landed(ids_v.at[j], i_ss.at[j], i_rs.at[j])
             to_smem = pltpu.make_async_copy(ids_v, ids_s, lsem.at[6])
             to_smem.start()
             to_smem.wait()
+            for sub in range(2):
+                y_step(4, sub)
             for t in range(5):
                 for way in range(2):
                     for sub in range(2):
@@ -314,7 +328,8 @@
                 serve(g, 2 * g - 1, 2)
                 return carry
 
-            lax.fori_loop(1, 5, serve_pair, 0)
+            lax.fori_loop(1, 4, serve_pair, 0)
+    serve(4, 7, 2)
     serve(5, 9, 2)
     serve(6, 11, 1)
     merge(0, 0, 1)
@@ -362,8 +377,8 @@
             pltpu.VMEM((NX, NZ, BLOCK, HD), BF),
             pltpu.VMEM((NX, NZ, RR, HD), BF),
             pltpu.VMEM((NX, NZ, RR, HD), BF),
-            pltpu.VMEM((NX, NZ, 2), jnp.int32),
-            pltpu.SMEM((NX, NZ, 2), jnp.int32),
+            pltpu.VMEM((NX, 2, NZ), jnp.int32),
+            pltpu.SMEM((NX, 2, NZ), jnp.int32),
             dma((7,)),
             dma((2, 6, 2)),
             dma((2, 6, 2)),
@@ -384,7 +399,7 @@
             collective_id=0, has_side_effects=True, vmem_limit_bytes=56 * 1024 * 1024
         ),
     )(
-        hidden, norm_gain.reshape(1, D), query_weight, key_weight, value_weight, bank, neighbour_ids
+        hidden, norm_gain.reshape(1, D), query_weight, key_weight, value_weight, bank, neighbour_ids.T
     )
 
 

time: 107 us -> 96.1 us (0.90)
  Pallas kernels: 103 us -> 93.4 us
  local copies, waits for them, and re-layouts: 3.13 us -> 1.77 us
    pallas_call x1, Pallas kernels: 103 us -> 93.4 us  [per_device(): pl.pallas_call(kernel, out_shape=jax.ShapeDtypeStruct((NZ * BLOCK, width)...]
    unnamed x2 -> x1, local copies, waits for them, and re-layouts: 3.13 us -> 1.77 us
where the time goes in v2:
time: 96.1 us; the launch traced here: 95.1 us
  Pallas kernels  93.4 us (97%)
  local copies, waits for them, and re-layouts  1.77 us (2%)
    pallas_call x1, Pallas kernels, per_device(): pl.pallas_call(kernel, out_shape=jax.ShapeDtypeStruct((NZ * BLOCK, width)...  93.4 us

profile of v2, /device:TPU:1, one launch (start us, length us, event | category | flops | bytes accessed | tf_op | source)
XLA Modules:
  0.0 95.1 jit_solution(15230283721154467750)
XLA Ops:
  0.0 93.4 %shard_map.73 = bf16[768,256]{1,0:T(8,128)(2,1)} custom-call(bf16[64,4096]{1,0:T(8,128)(2,1)} %hidden.1, f32[1,4096]{1,0:T(1,128)} %bitcast.2, bf16[4096,256]{1,0:T(8,128)(2,1)} %wq.1, bf16[4096,256]{1,0:T(8,128)(2,1)} %wk.1, bf16[4096,256]{1,0:T(8,128)(2,1)} %wv.1, bf16[4,128,4096]{2,1,0:T(8,128)(2,1)} %bank.1, s32[2,12]{1,0:T(2,128)} %bitcast.3), custom_call_target="tpu_custom_call" | custom-call | tf_op jit(solution)/shard_map/pallas_call | solution.py:362
  93.4 1.8 %copy.9 = bf16[768,256]{1,0:T(8,128)(2,1)} copy(bf16[768,256]{1,0:T(8,128)(2,1)} %shard_map.73) | data formatting | bytes 786432

commit v3 on v2

v3 whole, which is shorter than its diff:
```python
import jax
import jax.numpy as jnp
from jax import lax
from jax.experimental import pallas as pl
from jax.experimental.pallas import tpu as pltpu
from jax.sharding import PartitionSpec as P

HD = 128
BLOCK = 64
NBR = 128
EPS = 1e-6
NX, NY, NZ = 4, 8, 12
D = 4096
ROWS = 4
NEG = -1e30
RR = 80
MESH = pl.DeviceIdType.MESH
BF = jnp.bfloat16
F32 = jnp.float32


GROUPS = ((0, 1), (1, 2), (3, 2), (5, 1), (6, 2), (8, 2), (10, 2))
HALF = NZ // 2


def kernel(
    hidden, gain, wq, wk, wv, bank, ids, out,
    hid_v, wq_v, w2_v, wk_v, wv_v, bank_v, zb, kv, kvs, qq, q2, q_in, r_out, r_in, ids_v, ids_s,
    lsem, s_sem, z_rs, y_rs, x_rs, b_rs, q_rs, r_rs, i_rs, w0_rs, wy_rs, wx_rs, wb_rs, f_rs,
    out_v, o_sem,
):
    db = lax.axis_index("db")
    z = lax.axis_index("mp")
    c = db % 2
    x = (db // 2) % NX
    y = db // (2 * NX)
    x0 = x % 2
    x1 = x // 2
    turn = 1 - 2 * c

    def dev(yy, xx, cc, zz):
        return {"db": (yy * NX + xx) * 2 + cc, "mp": zz}

    xs = (x, x + 1 - 2 * x0, (x + 2) % NX, NX - 1 - x)
    z_dev = (dev(y, x, c, (z + NZ - turn) % NZ), dev(y, x, c, (z + NZ + turn) % NZ))
    far = dev(y, x, c, (z + HALF) % NZ)
    y_dev = tuple(dev((y + d) % NY, x, c, z) for d in range(NY))
    x_dev = tuple(dev(y, xx, c, z) for xx in xs)
    ring = (dev(y, (x + 1) % NX, c, z), dev(y, (x + NX - 1) % NX, c, z))
    sib = dev(y, x, 1 - c, z)
    peers = z_dev + (far,) + y_dev[1:] + x_dev[1:] + (sib,)

    loads = [
        pltpu.make_async_copy(a, b, lsem.at[n])
        for n, (a, b) in enumerate(
            ((hidden, hid_v), (wq, wq_v), (bank, bank_v), (wk, wk_v), (wv, wv_v), (ids, ids_v.at[0]))
        )
    ]
    for load in loads:
        load.start()
    barrier = pltpu.get_barrier_semaphore()
    for peer in peers:
        pl.semaphore_signal(barrier, inc=1, device_id=peer, device_id_type=MESH)

    def copy(src, dst, ss, rs, to):
        return pltpu.make_async_remote_copy(
            src_ref=src, dst_ref=dst, send_sem=ss, recv_sem=rs, device_id=to, device_id_type=MESH
        )

    def send(src, dst, family, rs, to):
        copy(src, dst, s_sem.at[family], rs, to).start()

    def landed(dst, rs):
        copy(dst, dst, s_sem.at[0], rs, sib).wait_recv()

    def all_sent(like, family):
        copy(like, like, s_sem.at[family], s_sem.at[family], sib).wait_send()

    loads[0].wait()

    def norm_rows(n, carry):
        rows = pl.ds(pl.multiple_of(n * 16, 16), 16)
        stream = hid_v[rows, :].astype(F32)
        factor = lax.rsqrt(jnp.mean(stream * stream, axis=-1, keepdims=True) + EPS)
        zb[0, rows, :] = (stream * factor * gain[...]).astype(BF)
        return carry

    lax.fori_loop(0, BLOCK // 16, norm_rows, 0)
    loads[1].wait()
    pl.semaphore_wait(barrier, len(peers))

    def w_rows(first, count):
        return w2_v.at[pl.ds(pl.multiple_of(first, 64), count)]

    def w_slice(yy):
        return w_rows(x * 1024 + c * 512 + yy * 64, 64)

    send(
        wq_v.at[pl.ds(pl.multiple_of(x * 1024 + c * 512 + y * 64, 64), 64)], w_slice(y),
        0, w0_rs.at[0], far,
    )

    def w_along_y():
        landed(w_slice(y), w0_rs.at[0])
        for d in (1, 7, 2, 6, 3, 5, 4):
            send(w_slice(y), w_slice(y), 1, wy_rs.at[0], y_dev[d])

    def w_block(xx, cc):
        return w_rows(xx * 1024 + cc * 512, 512)

    def w_half(xx, cc, half):
        return w_rows(xx * 1024 + cc * 512 + half * 256, 256)

    def w_along_x():
        landed(w2_v.at[pl.ds(0, 64 * (NY - 1))], wy_rs.at[0])
        own_block = w_block(x, c)
        for way in range(2):
            send(own_block, own_block, 2, wx_rs.at[way, 0], ring[way])
        send(own_block, own_block, 3, wb_rs.at[0], sib)

    def w_from(way):
        return (x + NX - 1) % NX if way == 0 else (x + 1) % NX

    def w_on():
        for way in range(2):
            block = w_block(w_from(way), c)
            landed(block, wx_rs.at[way, 0])
            half = w_half(w_from(way), c, way)
            send(half, half, 2, wx_rs.at[way, 1], ring[way])
            send(block, block, 3, wb_rs.at[0], sib)

    def w_last():
        for way in range(2):
            half = w_half((x + 2) % NX, c, way)
            landed(half, wx_rs.at[way, 1])
            send(half, half, 3, wb_rs.at[0], sib)

    def w_whole():
        landed(w2_v.at[pl.ds(0, D // 2)], wb_rs.at[0])

    STEPS = (3, 2)

    def z_part(slot, sub):
        return zb.at[slot, pl.ds(sub * 32, 32), :]

    def z_slot(way, s):
        return 0 if s == 0 else 2 * s - 1 + way

    def z_send(way, s, sub):
        send(
            z_part(z_slot(way, s), sub), z_part(z_slot(way, s + 1), sub),
            4, z_rs.at[way, s, sub], z_dev[way],
        )

    def z_step(s, sub):
        for way in range(2):
            if s <= STEPS[way]:
                landed(z_part(z_slot(way, s), sub), z_rs.at[way, s - 1, sub])
                if s < STEPS[way]:
                    z_send(way, s, sub)

    for sub in range(2):
        for way in range(2):
            z_send(way, 0, sub)

    loads[5].wait()
    for j in (1, 2, 3):
        send(ids_v.at[0], ids_v.at[j], 5, i_rs.at[0], x_dev[j])

    def unit(yy, cc, bit):
        return ((yy * 2 + cc) * 2 + bit) * ROWS

    own = unit(y, c, x0)

    def project(which):
        weight = (wk_v, wv_v)[which]

        def rows_of(n, carry):
            got = jnp.dot(
                bank_v[pl.ds(n * 2, 2)].reshape(2 * NBR, D), weight[...], preferred_element_type=F32
            )
            low, high = got[:, :HD], got[:, HD:]
            mine = jnp.where(x0 == 0, low, high).astype(BF)
            other = jnp.where(x0 == 0, high, low).astype(BF)
            for a in range(2):
                kv[which, own + n * 2 + a] = mine[a * NBR : (a + 1) * NBR]
                kvs[which, n * 2 + a] = other[a * NBR : (a + 1) * NBR]
            return carry

        lax.fori_loop(0, ROWS // 2, rows_of, 0)

    def y_at(way, s):
        return (y + NY - s) % NY if way == 0 else (y + s) % NY

    def kv_part(yy, cc, sub):
        return kv.at[sub % 2, pl.ds(unit(yy, cc, x0 if sub < 2 else 1 - x0), ROWS)]

    def y_send(way, s, sub):
        part = kv_part(y_at(way, s), c, sub)
        send(part, part, 6, y_rs.at[way, s, sub], y_dev[1 if way == 0 else NY - 1])

    def b_send(way, s, sub):
        part = kv_part(y_at(way, s), c, sub)
        send(part, part, 7, b_rs.at[0], sib)

    def y_needed(way, s, sub):
        return s < 4 or sub // 2 == way

    def y_first(sub):
        for way in range(2):
            y_send(way, 0, sub)
        b_send(0, 0, sub)

    def y_step(s, *subs, ways=(0, 1)):
        for sub in subs:
            for way in ways:
                if y_needed(way, s, sub):
                    part = kv_part(y_at(way, s), c, sub)
                    landed(part, y_rs.at[way, s - 1, sub])
                    if s < 4 and y_needed(way, s + 1, sub):
                        y_send(way, s, sub)
                    b_send(way, s, sub)

    def neighbour(which):
        landed(kv_part(y, c, 2 + which), x_rs.at[which])
        y_first(2 + which)

    scale = HD ** (-0.5)

    def store_queries(got, ref, first, count):
        got = got * scale
        low, high = got[:, :HD], got[:, HD:]
        mine = jnp.where(x0 == 0, low, high).astype(BF)
        other = jnp.where(x0 == 0, high, low).astype(BF)
        for a in range(count):
            ref[first + a, 0] = mine[a * BLOCK : (a + 1) * BLOCK]
            ref[first + a, 1] = other[a * BLOCK : (a + 1) * BLOCK]

    def rows_of_slots(first, count):
        return zb[first : first + count].reshape(count * BLOCK, D)

    def q_along_x(g):
        first, count = GROUPS[g]
        for j in (2, 1, 3):
            send(
                qq.at[pl.ds(first, count), 0 if j == 2 else 1], q_in.at[j, pl.ds(first, count)],
                9, q_rs.at[g], x_dev[j],
            )

    def queries(g):
        first, count = GROUPS[g]
        got = jnp.dot(rows_of_slots(first, count), wq_v[...], preferred_element_type=F32)
        store_queries(got, qq, first, count)
        q_along_x(g)

    def far_queries(n):
        got = jnp.dot(rows_of_slots(2 * n, 2), w2_v[...], preferred_element_type=F32)
        store_queries(got, q2, 2 * n, 2)
        send(
            q2.at[pl.ds(2 * n, 2)], qq.at[pl.ds(HALF + 2 * n, 2)], 10, f_rs.at[n], far
        )

    def relay(n):
        landed(qq.at[pl.ds(HALF + 2 * n, 2)], f_rs.at[n])
        q_along_x(4 + n)

    def block_of(slot):
        u = slot % HALF
        sign = turn * (2 * (u % 2) - 1)
        return (z + NZ + HALF * (slot // HALF) + sign * ((u + 1) // 2)) % NZ

    diag = lax.broadcasted_iota(jnp.int32, (BLOCK, HD), 0) == lax.broadcasted_iota(
        jnp.int32, (BLOCK, HD), 1
    )
    row_no = lax.broadcasted_iota(jnp.int32, (16, HD), 0)

    lane = lax.broadcasted_iota(jnp.int32, (1, 2 * NBR), 1)

    def attend(items):
        loaded = []
        for j, slot in items:
            block = block_of(slot)
            rows, bias = [], []
            for k in range(2):
                nbr = ids_s[j, k, block]
                shard = nbr // ROWS
                col = (shard // 2) % NX
                rows.append(
                    ((shard // (2 * NX) * 2 + shard % 2) * 2 + col % 2) * ROWS + nbr % ROWS
                )
                bias.append(jnp.where(col // 2 == x1, 0.0, NEG))
            loaded.append((
                qq[slot, 0] if j == 0 else q_in[j, slot],
                jnp.concatenate([kv[0, rows[0]], kv[0, rows[1]]], axis=0),
                jnp.concatenate([kv[1, rows[0]], kv[1, rows[1]]], axis=0),
                jnp.where(lane < NBR, bias[0], bias[1]),
            ))
        scores = [
            lax.dot_general(q, keys, (((1,), (1,)), ((), ())), preferred_element_type=F32) + bias
            for q, keys, _, bias in loaded
        ]
        expo = [jnp.exp(s) for s in scores]
        denom = [jnp.sum(e, axis=-1, keepdims=True) for e in expo]
        down = [jnp.where(d > 1.0, 0.0625, 1.0) for d in denom]
        inverse = [jnp.where(d > 0.0, 1.0 / (d * w), 0.0) for d, w in zip(denom, down)]
        probs = [(e * w * v).astype(BF) for e, w, v in zip(expo, down, inverse)]
        parts = [
            jnp.dot(p, values, preferred_element_type=F32)
            for p, (_, _, values, _) in zip(probs, loaded)
        ]
        for (j, slot), part, d in zip(items, parts, denom):
            r_out[j, slot, 0:BLOCK, :] = part.astype(BF)
            total = jnp.sum(jnp.where(diag, d, 0.0), axis=0, keepdims=True)
            hi = total.astype(BF).astype(F32)
            mid = (total - hi).astype(BF).astype(F32)
            lo = total - hi - mid
            packed = jnp.where(
                row_no == 0, hi, jnp.where(row_no == 1, mid, jnp.where(row_no == 2, lo, 0.0))
            )
            r_out[j, slot, BLOCK:RR, :] = packed.astype(BF)

    def r_copy(j, g, first, count):
        return copy(
            r_out.at[j, pl.ds(first, count)], r_in.at[j, pl.ds(first, count)],
            s_sem.at[11], r_rs.at[g], x_dev[j],
        )

    def serve(parts):
        for g, first, count in parts:
            landed(q_in.at[pl.ds(1, 3), pl.ds(first, count)], q_rs.at[g])
        attend([
            (j, first + a) for j in (1, 2, 3, 0) for _, first, count in parts for a in range(count)
        ])
        for g, first, count in parts:
            for j in (1, 2, 3):
                r_copy(j, g, first, count).start()

    ones = jnp.ones((16, HD), BF)

    def sum_of(ref, j, slot):
        spread = lax.dot_general(
            ref[j, slot, BLOCK:RR, :], ones, (((0,), (0,)), ((), ())), preferred_element_type=F32
        )
        return spread[:BLOCK]

    def out_copy(slot):
        rows = pl.ds(pl.multiple_of(block_of(slot) * BLOCK, BLOCK), BLOCK)
        return pltpu.make_async_copy(out_v.at[slot], out.at[rows], o_sem.at[0])

    def merge(parts):
        for g, first, count in parts:
            landed(r_in.at[pl.ds(1, 3), pl.ds(first, count)], r_rs.at[g])
        slots = [first + a for _, first, count in parts for a in range(count)]
        todo = [
            (slot, head, pair)
            for slot in slots
            for head, pair in ((x0, ((r_out, 0), (r_in, 2))), (1 - x0, ((r_in, 1), (r_in, 3))))
        ]
        sums = [[sum_of(ref, j, slot) for ref, j in pair] for slot, _, pair in todo]
        vals = [
            [ref[j, slot, 0:BLOCK, :].astype(F32) for ref, j in pair] for slot, _, pair in todo
        ]
        for (slot, head, _), (la, lb), (va, vb) in zip(todo, sums, vals):
            both = jnp.where(la + lb > 0.0, la + lb, 1.0)
            mixed = (la / both) * va + (lb / both) * vb
            out_v[slot, :, pl.ds(pl.multiple_of(head * HD, HD), HD)] = mixed.astype(BF)
        for slot in slots:
            out_copy(slot).start()

    loads[2].wait()
    loads[3].wait()
    project(0)
    y_first(0)
    send(kvs.at[0], kv.at[0, pl.ds(own, ROWS)], 8, x_rs.at[0], x_dev[1])
    loads[4].wait()
    project(1)
    y_first(1)
    send(kvs.at[1], kv.at[1, pl.ds(own, ROWS)], 8, x_rs.at[1], x_dev[1])
    queries(0)
    w_along_y()
    z_step(1, 0)
    w_along_x()
    y_step(1, 0)
    neighbour(0)
    y_step(1, 1)
    neighbour(1)
    landed(ids_v.at[pl.ds(1, 3)], i_rs.at[0])
    to_smem = pltpu.make_async_copy(ids_v, ids_s, lsem.at[6])
    to_smem.start()
    z_step(1, 1)
    queries(1)
    z_step(2, 0)
    w_on()
    w_last()
    z_step(2, 1)
    queries(2)
    y_step(1, 2, 3)
    y_step(2, 0, 1)
    w_whole()
    far_queries(0)
    far_queries(1)
    z_step(3, 0)
    z_step(3, 1)
    queries(3)
    far_queries(2)
    y_step(2, 2, 3)
    y_step(3, 0, 1)
    relay(0)
    relay(1)
    y_step(3, 2, 3, ways=(1,))
    relay(2)
    y_step(3, 2, 3, ways=(0,))
    to_smem.wait()
    y_step(4, 0, 2, 1, 3)
    landed(kv.at[0], b_rs.at[0])

    serve([(0, 0, 1), (3, 5, 1)])

    def serve_near(n, carry):
        serve([(1 + n, 1 + 2 * n, 2)])
        return carry

    def serve_away(n, carry):
        serve([(4 + n, HALF + 2 * n, 2)])
        return carry

    lax.fori_loop(0, 2, serve_near, 0)
    lax.fori_loop(0, 3, serve_away, 0)
    merge([(0, 0, 1), (3, 5, 1)])

    def merge_near(n, carry):
        merge([(1 + n, 1 + 2 * n, 2)])
        return carry

    def merge_away(n, carry):
        merge([(4 + n, HALF + 2 * n, 2)])
        return carry

    lax.fori_loop(0, 2, merge_near, 0)
    lax.fori_loop(0, 3, merge_away, 0)

    for family, like in enumerate((
        w2_v.at[pl.ds(0, 64)],
        w2_v.at[pl.ds(0, 64 * (NY - 1))],
        w2_v.at[pl.ds(0, 1536)],
        w2_v.at[pl.ds(0, D // 2)],
        zb.at[pl.ds(0, 5)],
        ids_v.at[pl.ds(1, 3)],
        kv.at[0, pl.ds(0, 112)],
        kv.at[0],
        kvs,
        q_in.at[pl.ds(1, 3)],
        q2,
        r_in.at[pl.ds(1, 3)],
    )):
        all_sent(like, family)
    pltpu.make_async_copy(out_v, out_v, o_sem.at[0]).wait()


def per_device(hidden, norm_gain, query_weight, key_weight, value_weight, bank, neighbour_ids):
    hbm = pl.BlockSpec(memory_space=pl.ANY)
    vmem = pl.BlockSpec(memory_space=pltpu.VMEM)
    dma = pltpu.SemaphoreType.DMA
    width = query_weight.shape[1]
    return pl.pallas_call(
        kernel,
        out_shape=jax.ShapeDtypeStruct((NZ * BLOCK, width), BF),
        in_specs=[hbm, vmem, hbm, hbm, hbm, hbm, hbm],
        out_specs=hbm,
        scratch_shapes=[
            pltpu.VMEM((BLOCK, D), BF),
            pltpu.VMEM((D, width), BF),
            pltpu.VMEM((D, width), BF),
            pltpu.VMEM((D, width), BF),
            pltpu.VMEM((D, width), BF),
            pltpu.VMEM((ROWS, NBR, D), BF),
            pltpu.VMEM((HALF, BLOCK, D), BF),
            pltpu.VMEM((2, NY * 2 * 2 * ROWS, NBR, HD), BF),
            pltpu.VMEM((2, ROWS, NBR, HD), BF),
            pltpu.VMEM((NZ, 2, BLOCK, HD), BF),
            pltpu.VMEM((HALF, 2, BLOCK, HD), BF),
            pltpu.VMEM((NX, NZ, BLOCK, HD), BF),
            pltpu.VMEM((NX, NZ, RR, HD), BF),
            pltpu.VMEM((NX, NZ, RR, HD), BF),
            pltpu.VMEM((NX, 2, NZ), jnp.int32),
            pltpu.SMEM((NX, 2, NZ), jnp.int32),
            dma((7,)),
            dma((12,)),
            dma((2, 3, 2)),
            dma((2, 4, 4)),
            dma((2,)),
            dma((1,)),
            dma((7,)),
            dma((7,)),
            dma((1,)),
            dma((1,)),
            dma((1,)),
            dma((2, 2)),
            dma((1,)),
            dma((3,)),
            pltpu.VMEM((NZ, BLOCK, width), BF),
            dma((1,)),
        ],
        compiler_params=pltpu.CompilerParams(
            collective_id=0, has_side_effects=True, vmem_limit_bytes=56 * 1024 * 1024
        ),
    )(
        hidden, norm_gain.reshape(1, D), query_weight, key_weight, value_weight, bank, neighbour_ids.T
    )


def solution(mesh):
    placed = (
        P(("db", "mp"), None),
        P(),
        P(None, "mp"),
        P(None, "mp"),
        P(None, "mp"),
        P("db", None, None),
        P("db", None),
    )
    return jax.shard_map(
        per_device, mesh=mesh, in_specs=placed, out_specs=P("db", "mp"), check_vma=False
    )
```

time: 96.1 us -> 90.2 us (0.939)
  Pallas kernels: 93.4 us -> 88.2 us
    pallas_call x1, Pallas kernels: 93.4 us -> 88.2 us  [per_device(): pl.pallas_call(kernel, out_shape=jax.ShapeDtypeStruct((NZ * BLOCK, width)...]
where the time goes in v3:
time: 90.2 us; the launch traced here: 90 us
  Pallas kernels  88.2 us (98%)
  local copies, waits for them, and re-layouts  1.77 us (2%)
    pallas_call x1, Pallas kernels, per_device(): pl.pallas_call(kernel, out_shape=jax.ShapeDtypeStruct((NZ * BLOCK, width)...  88.2 us

profile of v3, /device:TPU:1, one launch (start us, length us, event | category | flops | bytes accessed | tf_op | source)
XLA Modules:
  0.0 90.0 jit_solution(10099525616459993581)
XLA Ops:
  0.0 88.2 %shard_map.73 = bf16[768,256]{1,0:T(8,128)(2,1)} custom-call(bf16[64,4096]{1,0:T(8,128)(2,1)} %hidden.1, f32[1,4096]{1,0:T(1,128)} %bitcast.2, bf16[4096,256]{1,0:T(8,128)(2,1)} %wq.1, bf16[4096,256]{1,0:T(8,128)(2,1)} %wk.1, bf16[4096,256]{1,0:T(8,128)(2,1)} %wv.1, bf16[4,128,4096]{2,1,0:T(8,128)(2,1)} %bank.1, s32[2,12]{1,0:T(2,128)} %bitcast.3), custom_call_target="tpu_custom_call" | custom-call | tf_op jit(solution)/shard_map/pallas_call | solution.py:465
  88.2 1.8 %copy.9 = bf16[768,256]{1,0:T(8,128)(2,1)} copy(bf16[768,256]{1,0:T(8,128)(2,1)} %shard_map.73) | data formatting | bytes 786432

commit v4 on v3

--- a/solution.py
+++ b/solution.py
@@ -13,7 +13,7 @@
 D = 4096
 ROWS = 4
 NEG = -1e30
-RR = 80
+RR = 144
 MESH = pl.DeviceIdType.MESH
 BF = jnp.bfloat16
 F32 = jnp.float32
@@ -44,17 +44,26 @@
     xs = (x, x + 1 - 2 * x0, (x + 2) % NX, NX - 1 - x)
     z_dev = (dev(y, x, c, (z + NZ - turn) % NZ), dev(y, x, c, (z + NZ + turn) % NZ))
     far = dev(y, x, c, (z + HALF) % NZ)
-    y_dev = tuple(dev((y + d) % NY, x, c, z) for d in range(NY))
+    y_dev = (dev((y + 1) % NY, x, c, z), dev((y + NY - 1) % NY, x, c, z))
+    away = 2 * (y % 2) - 1
+    y_three = tuple(dev((y + NY + away * d) % NY, x, c, z) for d in (1, 2, 3))
     x_dev = tuple(dev(y, xx, c, z) for xx in xs)
     ring = (dev(y, (x + 1) % NX, c, z), dev(y, (x + NX - 1) % NX, c, z))
     sib = dev(y, x, 1 - c, z)
-    peers = z_dev + (far,) + y_dev[1:] + x_dev[1:] + (sib,)
-
+    peers = z_dev + (far,) + tuple(dev((y + d) % NY, x, c, z) for d in (1, 2, 3, 5, 6, 7)) + x_dev[1:] + (sib,)
+
+    half = ROWS // 2
     loads = [
         pltpu.make_async_copy(a, b, lsem.at[n])
-        for n, (a, b) in enumerate(
-            ((hidden, hid_v), (wq, wq_v), (bank, bank_v), (wk, wk_v), (wv, wv_v), (ids, ids_v.at[0]))
-        )
+        for n, (a, b) in enumerate((
+            (hidden, hid_v),
+            (ids, ids_v.at[0]),
+            (wk, wk_v),
+            (bank.at[pl.ds(0, half)], bank_v.at[pl.ds(0, half)]),
+            (bank.at[pl.ds(half, half)], bank_v.at[pl.ds(half, half)]),
+            (wv, wv_v),
+            (wq, wq_v),
+        ))
     ]
     for load in loads:
         load.start()
@@ -76,34 +85,30 @@
     def all_sent(like, family):
         copy(like, like, s_sem.at[family], s_sem.at[family], sib).wait_send()
 
-    loads[0].wait()
-
-    def norm_rows(n, carry):
-        rows = pl.ds(pl.multiple_of(n * 16, 16), 16)
-        stream = hid_v[rows, :].astype(F32)
-        factor = lax.rsqrt(jnp.mean(stream * stream, axis=-1, keepdims=True) + EPS)
-        zb[0, rows, :] = (stream * factor * gain[...]).astype(BF)
-        return carry
-
-    lax.fori_loop(0, BLOCK // 16, norm_rows, 0)
-    loads[1].wait()
-    pl.semaphore_wait(barrier, len(peers))
+    def norm():
+        def norm_rows(n, carry):
+            rows = pl.ds(pl.multiple_of(n * 16, 16), 16)
+            stream = hid_v[rows, :].astype(F32)
+            factor = lax.rsqrt(jnp.mean(stream * stream, axis=-1, keepdims=True) + EPS)
+            zb[0, rows, :] = (stream * factor * gain[...]).astype(BF)
+            return carry
+
+        lax.fori_loop(0, BLOCK // 16, norm_rows, 0)
 
     def w_rows(first, count):
         return w2_v.at[pl.ds(pl.multiple_of(first, 64), count)]
 
     def w_slice(yy):
-        return w_rows(x * 1024 + c * 512 + yy * 64, 64)
-
-    send(
-        wq_v.at[pl.ds(pl.multiple_of(x * 1024 + c * 512 + y * 64, 64), 64)], w_slice(y),
-        0, w0_rs.at[0], far,
-    )
+        return w_rows(x * 1024 + c * 512 + yy // 2 * 128, 128)
+
+    def w_far():
+        first = pl.multiple_of(x * 1024 + c * 512 + y // 2 * 128, 128)
+        send(wq.at[pl.ds(first, 128)], w_slice(y), 0, w0_rs.at[0], far)
 
     def w_along_y():
         landed(w_slice(y), w0_rs.at[0])
-        for d in (1, 7, 2, 6, 3, 5, 4):
-            send(w_slice(y), w_slice(y), 1, wy_rs.at[0], y_dev[d])
+        for to in y_three:
+            send(w_slice(y), w_slice(y), 1, wy_rs.at[0], to)
 
     def w_block(xx, cc):
         return w_rows(xx * 1024 + cc * 512, 512)
@@ -112,7 +117,7 @@
         return w_rows(xx * 1024 + cc * 512 + half * 256, 256)
 
     def w_along_x():
-        landed(w2_v.at[pl.ds(0, 64 * (NY - 1))], wy_rs.at[0])
+        landed(w2_v.at[pl.ds(0, 3 * 128)], wy_rs.at[0])
         own_block = w_block(x, c)
         for way in range(2):
             send(own_block, own_block, 2, wx_rs.at[way, 0], ring[way])
@@ -159,35 +164,34 @@
                 if s < STEPS[way]:
                     z_send(way, s, sub)
 
-    for sub in range(2):
-        for way in range(2):
-            z_send(way, 0, sub)
-
-    loads[5].wait()
-    for j in (1, 2, 3):
-        send(ids_v.at[0], ids_v.at[j], 5, i_rs.at[0], x_dev[j])
+    def z_first():
+        for sub in range(2):
+            for way in range(2):
+                z_send(way, 0, sub)
 
     def unit(yy, cc, bit):
         return ((yy * 2 + cc) * 2 + bit) * ROWS
 
     own = unit(y, c, x0)
 
-    def project(which):
-        weight = (wk_v, wv_v)[which]
-
-        def rows_of(n, carry):
-            got = jnp.dot(
-                bank_v[pl.ds(n * 2, 2)].reshape(2 * NBR, D), weight[...], preferred_element_type=F32
-            )
-            low, high = got[:, :HD], got[:, HD:]
-            mine = jnp.where(x0 == 0, low, high).astype(BF)
-            other = jnp.where(x0 == 0, high, low).astype(BF)
-            for a in range(2):
-                kv[which, own + n * 2 + a] = mine[a * NBR : (a + 1) * NBR]
-                kvs[which, n * 2 + a] = other[a * NBR : (a + 1) * NBR]
-            return carry
-
-        lax.fori_loop(0, ROWS // 2, rows_of, 0)
+    def project(which, n):
+        got = jnp.dot(
+            bank_v[pl.ds(n * half, half)].reshape(half * NBR, D), (wk_v, wv_v)[which][...],
+            preferred_element_type=F32,
+        )
+        low, high = got[:, :HD], got[:, HD:]
+        mine = jnp.where(x0 == 0, low, high).astype(BF)
+        other = jnp.where(x0 == 0, high, low).astype(BF)
+        for a in range(half):
+            kv[which, own + n * half + a] = mine[a * NBR : (a + 1) * NBR]
+            kvs[which, n * half + a] = other[a * NBR : (a + 1) * NBR]
+
+    def pass_on(which, n):
+        part = kv.at[which, pl.ds(own + n * half, half)]
+        for way in range(2):
+            send(part, part, 6, y_rs.at[way, 0, which], y_dev[way])
+        send(kvs.at[which, pl.ds(n * half, half)], part, 8, x_rs.at[which], x_dev[1])
+        send(part, part, 7, b_rs.at[0], sib)
 
     def y_at(way, s):
         return (y + NY - s) % NY if way == 0 else (y + s) % NY
@@ -197,7 +201,7 @@
 
     def y_send(way, s, sub):
         part = kv_part(y_at(way, s), c, sub)
-        send(part, part, 6, y_rs.at[way, s, sub], y_dev[1 if way == 0 else NY - 1])
+        send(part, part, 6, y_rs.at[way, s, sub], y_dev[way])
 
     def b_send(way, s, sub):
         part = kv_part(y_at(way, s), c, sub)
@@ -269,14 +273,14 @@
         sign = turn * (2 * (u % 2) - 1)
         return (z + NZ + HALF * (slot // HALF) + sign * ((u + 1) // 2)) % NZ
 
-    diag = lax.broadcasted_iota(jnp.int32, (BLOCK, HD), 0) == lax.broadcasted_iota(
-        jnp.int32, (BLOCK, HD), 1
+    offset = lax.broadcasted_iota(jnp.int32, (BLOCK, HD), 1) - lax.broadcasted_iota(
+        jnp.int32, (BLOCK, HD), 0
     )
     row_no = lax.broadcasted_iota(jnp.int32, (16, HD), 0)
 
     lane = lax.broadcasted_iota(jnp.int32, (1, 2 * NBR), 1)
 
-    def attend(items):
+    def attend(pair, items):
         loaded = []
         for j, slot in items:
             block = block_of(slot)
@@ -308,140 +312,157 @@
             jnp.dot(p, values, preferred_element_type=F32)
             for p, (_, _, values, _) in zip(probs, loaded)
         ]
-        for (j, slot), part, d in zip(items, parts, denom):
-            r_out[j, slot, 0:BLOCK, :] = part.astype(BF)
-            total = jnp.sum(jnp.where(diag, d, 0.0), axis=0, keepdims=True)
+        for n in range(0, len(items), 2):
+            j = items[n][0]
+            total = jnp.zeros((1, HD), F32)
+            for a in range(2):
+                r_out[j, pair, a * BLOCK : (a + 1) * BLOCK, :] = parts[n + a].astype(BF)
+                total += jnp.sum(
+                    jnp.where(offset == a * BLOCK, denom[n + a], 0.0), axis=0, keepdims=True
+                )
             hi = total.astype(BF).astype(F32)
             mid = (total - hi).astype(BF).astype(F32)
             lo = total - hi - mid
             packed = jnp.where(
                 row_no == 0, hi, jnp.where(row_no == 1, mid, jnp.where(row_no == 2, lo, 0.0))
             )
-            r_out[j, slot, BLOCK:RR, :] = packed.astype(BF)
-
-    def r_copy(j, g, first, count):
-        return copy(
-            r_out.at[j, pl.ds(first, count)], r_in.at[j, pl.ds(first, count)],
-            s_sem.at[11], r_rs.at[g], x_dev[j],
-        )
-
-    def serve(parts):
+            r_out[j, pair, 2 * BLOCK : RR, :] = packed.astype(BF)
+
+    def serve(pair, slots, parts):
         for g, first, count in parts:
             landed(q_in.at[pl.ds(1, 3), pl.ds(first, count)], q_rs.at[g])
-        attend([
-            (j, first + a) for j in (1, 2, 3, 0) for _, first, count in parts for a in range(count)
-        ])
-        for g, first, count in parts:
-            for j in (1, 2, 3):
-                r_copy(j, g, first, count).start()
+        attend(pair, [(j, slot) for j in (1, 2, 3, 0) for slot in slots])
+        for j in (2, 1, 3):
+            send(r_out.at[j, pair], r_in.at[j, pair], 11, r_rs.at[pair], x_dev[j])
 
     ones = jnp.ones((16, HD), BF)
 
-    def sum_of(ref, j, slot):
-        spread = lax.dot_general(
-            ref[j, slot, BLOCK:RR, :], ones, (((0,), (0,)), ((), ())), preferred_element_type=F32
+    def sums_of(ref, j, pair):
+        return lax.dot_general(
+            ref[j, pair, 2 * BLOCK : RR, :], ones, (((0,), (0,)), ((), ())),
+            preferred_element_type=F32,
         )
-        return spread[:BLOCK]
 
     def out_copy(slot):
         rows = pl.ds(pl.multiple_of(block_of(slot) * BLOCK, BLOCK), BLOCK)
         return pltpu.make_async_copy(out_v.at[slot], out.at[rows], o_sem.at[0])
 
-    def merge(parts):
-        for g, first, count in parts:
-            landed(r_in.at[pl.ds(1, 3), pl.ds(first, count)], r_rs.at[g])
-        slots = [first + a for _, first, count in parts for a in range(count)]
-        todo = [
-            (slot, head, pair)
-            for slot in slots
-            for head, pair in ((x0, ((r_out, 0), (r_in, 2))), (1 - x0, ((r_in, 1), (r_in, 3))))
-        ]
-        sums = [[sum_of(ref, j, slot) for ref, j in pair] for slot, _, pair in todo]
-        vals = [
-            [ref[j, slot, 0:BLOCK, :].astype(F32) for ref, j in pair] for slot, _, pair in todo
-        ]
-        for (slot, head, _), (la, lb), (va, vb) in zip(todo, sums, vals):
+    def merge(pair, slots):
+        landed(r_in.at[pl.ds(1, 3), pair], r_rs.at[pair])
+        todo = ((x0, (r_out, 0), (r_in, 2)), (1 - x0, (r_in, 1), (r_in, 3)))
+        sums = [[sums_of(ref, j, pair) for ref, j in two] for _, *two in todo]
+        vals = [[ref[j, pair, 0 : 2 * BLOCK, :].astype(F32) for ref, j in two] for _, *two in todo]
+        for (head, _, _), (la, lb), (va, vb) in zip(todo, sums, vals):
             both = jnp.where(la + lb > 0.0, la + lb, 1.0)
-            mixed = (la / both) * va + (lb / both) * vb
-            out_v[slot, :, pl.ds(pl.multiple_of(head * HD, HD), HD)] = mixed.astype(BF)
+            mixed = ((la / both) * va + (lb / both) * vb).astype(BF)
+            columns = pl.ds(pl.multiple_of(head * HD, HD), HD)
+            for a, slot in enumerate(slots):
+                out_v[slot, :, columns] = mixed[a * BLOCK : (a + 1) * BLOCK]
         for slot in slots:
             out_copy(slot).start()
 
+    loads[0].wait()
+    norm()
+    pl.semaphore_wait(barrier, len(peers))
+    w_far()
+    z_first()
+    loads[1].wait()
+    for j in (1, 2, 3):
+        send(ids_v.at[0], ids_v.at[j], 5, i_rs.at[0], x_dev[j])
     loads[2].wait()
-    loads[3].wait()
-    project(0)
-    y_first(0)
-    send(kvs.at[0], kv.at[0, pl.ds(own, ROWS)], 8, x_rs.at[0], x_dev[1])
-    loads[4].wait()
-    project(1)
-    y_first(1)
-    send(kvs.at[1], kv.at[1, pl.ds(own, ROWS)], 8, x_rs.at[1], x_dev[1])
+
+    def keys(n, carry):
+        part = bank_v.at[pl.ds(n * half, half)]
+        pltpu.make_async_copy(part, part, lsem.at[3 + n]).wait()
+        project(0, n)
+        pass_on(0, n)
+        return carry
+
+    lax.fori_loop(0, 2, keys, 0)
+    loads[5].wait()
+
+    def values(n, carry):
+        project(1, n)
+        pass_on(1, n)
+        return carry
+
+    lax.fori_loop(0, 2, values, 0)
+    loads[6].wait()
     queries(0)
     w_along_y()
-    z_step(1, 0)
-    w_along_x()
     y_step(1, 0)
     neighbour(0)
     y_step(1, 1)
     neighbour(1)
     landed(ids_v.at[pl.ds(1, 3)], i_rs.at[0])
-    to_smem = pltpu.make_async_copy(ids_v, ids_s, lsem.at[6])
+    to_smem = pltpu.make_async_copy(ids_v, ids_s, lsem.at[7])
     to_smem.start()
+    z_step(1, 0)
+    w_along_x()
+    y_step(2, 0)
     z_step(1, 1)
     queries(1)
+    y_step(1, 2)
     z_step(2, 0)
+    y_step(2, 1)
     w_on()
+    y_step(1, 3)
     w_last()
     z_step(2, 1)
+    y_step(3, 0)
     queries(2)
-    y_step(1, 2, 3)
-    y_step(2, 0, 1)
     w_whole()
     far_queries(0)
     far_queries(1)
+    y_step(2, 2)
     z_step(3, 0)
+    y_step(3, 1)
     z_step(3, 1)
+    y_step(2, 3)
     queries(3)
     far_queries(2)
-    y_step(2, 2, 3)
-    y_step(3, 0, 1)
+    y_step(3, 2, ways=(1,))
+    y_step(4, 0)
+    y_step(3, 2, ways=(0,))
+    y_step(3, 3, ways=(1,))
     relay(0)
+    y_step(4, 1)
+    y_step(4, 2)
     relay(1)
-    y_step(3, 2, 3, ways=(1,))
+    y_step(3, 3, ways=(0,))
+    y_step(4, 3)
     relay(2)
-    y_step(3, 2, 3, ways=(0,))
     to_smem.wait()
-    y_step(4, 0, 2, 1, 3)
     landed(kv.at[0], b_rs.at[0])
-
-    serve([(0, 0, 1), (3, 5, 1)])
+    serve(0, (0, 5), [(0, 0, 1), (3, 5, 1)])
 
     def serve_near(n, carry):
-        serve([(1 + n, 1 + 2 * n, 2)])
+        serve(1 + n, (1 + 2 * n, 2 + 2 * n), [(1 + n, 1 + 2 * n, 2)])
         return carry
 
     def serve_away(n, carry):
-        serve([(4 + n, HALF + 2 * n, 2)])
+        first = HALF + 2 * n
+        serve(3 + n, (first, first + 1), [(4 + n, first, 2)])
         return carry
 
     lax.fori_loop(0, 2, serve_near, 0)
     lax.fori_loop(0, 3, serve_away, 0)
-    merge([(0, 0, 1), (3, 5, 1)])
+    merge(0, (0, 5))
 
     def merge_near(n, carry):
-        merge([(1 + n, 1 + 2 * n, 2)])
+        merge(1 + n, (1 + 2 * n, 2 + 2 * n))
         return carry
 
     def merge_away(n, carry):
-        merge([(4 + n, HALF + 2 * n, 2)])
+        merge(3 + n, (HALF + 2 * n, HALF + 1 + 2 * n))
         return carry
 
     lax.fori_loop(0, 2, merge_near, 0)
     lax.fori_loop(0, 3, merge_away, 0)
 
     for family, like in enumerate((
-        w2_v.at[pl.ds(0, 64)],
-        w2_v.at[pl.ds(0, 64 * (NY - 1))],
+        w2_v.at[pl.ds(0, 128)],
+        w2_v.at[pl.ds(0, 3 * 128)],
         w2_v.at[pl.ds(0, 1536)],
         w2_v.at[pl.ds(0, D // 2)],
         zb.at[pl.ds(0, 5)],
@@ -480,18 +501,18 @@
             pltpu.VMEM((NZ, 2, BLOCK, HD), BF),
             pltpu.VMEM((HALF, 2, BLOCK, HD), BF),
             pltpu.VMEM((NX, NZ, BLOCK, HD), BF),
-            pltpu.VMEM((NX, NZ, RR, HD), BF),
-            pltpu.VMEM((NX, NZ, RR, HD), BF),
+            pltpu.VMEM((NX, HALF, RR, HD), BF),
+            pltpu.VMEM((NX, HALF, RR, HD), BF),
             pltpu.VMEM((NX, 2, NZ), jnp.int32),
             pltpu.SMEM((NX, 2, NZ), jnp.int32),
-            dma((7,)),
+            dma((8,)),
             dma((12,)),
             dma((2, 3, 2)),
             dma((2, 4, 4)),
             dma((2,)),
             dma((1,)),
             dma((7,)),
-            dma((7,)),
+            dma((6,)),
             dma((1,)),
             dma((1,)),
             dma((1,)),

time: 90.2 us -> 86.3 us (0.957)
  the two profiles are of different devices: /device:TPU:1 before, /device:TPU:240 now
where the time goes in v4:
time: 86.3 us; the launch traced here: 86.1 us
  Pallas kernels  84.3 us (98%)
  local copies, waits for them, and re-layouts  1.77 us (2%)
    pallas_call x1, Pallas kernels, per_device(): pl.pallas_call(kernel, out_shape=jax.ShapeDtypeStruct((NZ * BLOCK, width)...  84.3 us
    unnamed x1, local copies, waits for them, and re-layouts  1.77 us

profile of v4, /device:TPU:240, one launch (start us, length us, event | category | flops | bytes accessed | tf_op | source)
XLA Modules:
  0.0 86.1 jit_solution(6982307030654036415)
XLA Ops:
  0.0 84.3 %shard_map.73 = bf16[768,256]{1,0:T(8,128)(2,1)} custom-call(bf16[64,4096]{1,0:T(8,128)(2,1)} %hidden.1, f32[1,4096]{1,0:T(1,128)} %bitcast.2, bf16[4096,256]{1,0:T(8,128)(2,1)} %wq.1, bf16[4096,256]{1,0:T(8,128)(2,1)} %wk.1, bf16[4096,256]{1,0:T(8,128)(2,1)} %wv.1, bf16[4,128,4096]{2,1,0:T(8,128)(2,1)} %bank.1, s32[2,12]{1,0:T(2,128)} %bitcast.3), custom_call_target="tpu_custom_call" | custom-call | tf_op jit(solution)/shard_map/pallas_call | solution.py:486
  84.3 1.8 %copy.9 = bf16[768,256]{1,0:T(8,128)(2,1)} copy(bf16[768,256]{1,0:T(8,128)(2,1)} %shard_map.73) | data formatting | bytes 786432

commit v5 on v4

--- a/solution.py
+++ b/solution.py
@@ -13,7 +13,6 @@
 D = 4096
 ROWS = 4
 NEG = -1e30
-RR = 144
 MESH = pl.DeviceIdType.MESH
 BF = jnp.bfloat16
 F32 = jnp.float32
@@ -27,7 +26,7 @@
     hidden, gain, wq, wk, wv, bank, ids, out,
     hid_v, wq_v, w2_v, wk_v, wv_v, bank_v, zb, kv, kvs, qq, q2, q_in, r_out, r_in, ids_v, ids_s,
     lsem, s_sem, z_rs, y_rs, x_rs, b_rs, q_rs, r_rs, i_rs, w0_rs, wy_rs, wx_rs, wb_rs, f_rs,
-    out_v, o_sem,
+    gain_v, l_out, l_in, l_rs,
 ):
     db = lax.axis_index("db")
     z = lax.axis_index("mp")
@@ -57,6 +56,7 @@
         pltpu.make_async_copy(a, b, lsem.at[n])
         for n, (a, b) in enumerate((
             (hidden, hid_v),
+            (gain, gain_v),
             (ids, ids_v.at[0]),
             (wk, wk_v),
             (bank.at[pl.ds(0, half)], bank_v.at[pl.ds(0, half)]),
@@ -90,7 +90,7 @@
             rows = pl.ds(pl.multiple_of(n * 16, 16), 16)
             stream = hid_v[rows, :].astype(F32)
             factor = lax.rsqrt(jnp.mean(stream * stream, axis=-1, keepdims=True) + EPS)
-            zb[0, rows, :] = (stream * factor * gain[...]).astype(BF)
+            zb[0, rows, :] = (stream * factor * gain_v[...]).astype(BF)
             return carry
 
         lax.fori_loop(0, BLOCK // 16, norm_rows, 0)
@@ -320,13 +320,7 @@
                 total += jnp.sum(
                     jnp.where(offset == a * BLOCK, denom[n + a], 0.0), axis=0, keepdims=True
                 )
-            hi = total.astype(BF).astype(F32)
-            mid = (total - hi).astype(BF).astype(F32)
-            lo = total - hi - mid
-            packed = jnp.where(
-                row_no == 0, hi, jnp.where(row_no == 1, mid, jnp.where(row_no == 2, lo, 0.0))
-            )
-            r_out[j, pair, 2 * BLOCK : RR, :] = packed.astype(BF)
+            l_out[j, pair // 3, pl.ds(pair % 3, 1), :] = total
 
     def serve(pair, slots, parts):
         for g, first, count in parts:
@@ -337,49 +331,59 @@
 
     ones = jnp.ones((16, HD), BF)
 
-    def sums_of(ref, j, pair):
+    def send_sums(third):
+        for j in (2, 1, 3):
+            send(l_out.at[j, third], l_in.at[j, third], 12, l_rs.at[third], x_dev[j])
+
+    def column(row):
+        hi = row.astype(BF).astype(F32)
+        mid = (row - hi).astype(BF).astype(F32)
+        lo = row - hi - mid
+        terms = jnp.where(
+            row_no == 0, hi, jnp.where(row_no == 1, mid, jnp.where(row_no == 2, lo, 0.0))
+        )
         return lax.dot_general(
-            ref[j, pair, 2 * BLOCK : RR, :], ones, (((0,), (0,)), ((), ())),
-            preferred_element_type=F32,
-        )
-
-    def out_copy(slot):
-        rows = pl.ds(pl.multiple_of(block_of(slot) * BLOCK, BLOCK), BLOCK)
-        return pltpu.make_async_copy(out_v.at[slot], out.at[rows], o_sem.at[0])
+            terms.astype(BF), ones, (((0,), (0,)), ((), ())), preferred_element_type=F32
+        )
 
     def merge(pair, slots):
         landed(r_in.at[pl.ds(1, 3), pair], r_rs.at[pair])
-        todo = ((x0, (r_out, 0), (r_in, 2)), (1 - x0, (r_in, 1), (r_in, 3)))
-        sums = [[sums_of(ref, j, pair) for ref, j in two] for _, *two in todo]
-        vals = [[ref[j, pair, 0 : 2 * BLOCK, :].astype(F32) for ref, j in two] for _, *two in todo]
-        for (head, _, _), (la, lb), (va, vb) in zip(todo, sums, vals):
-            both = jnp.where(la + lb > 0.0, la + lb, 1.0)
-            mixed = ((la / both) * va + (lb / both) * vb).astype(BF)
+        todo = (
+            (x0, (r_out, l_out, 0), (r_in, l_in, 2)),
+            (1 - x0, (r_in, l_in, 1), (r_in, l_in, 3)),
+        )
+        weights, vals = [], []
+        for _, *two in todo:
+            la, lb = (sums[j, pair // 3, pl.ds(pair % 3, 1), :] for _, sums, j in two)
+            weights.append(column(la / jnp.where(la + lb > 0.0, la + lb, 1.0)))
+            vals.append([ref[j, pair].astype(F32) for ref, _, j in two])
+        for (head, _, _), wa, (va, vb) in zip(todo, weights, vals):
+            mixed = (wa * va + (1.0 - wa) * vb).astype(BF)
             columns = pl.ds(pl.multiple_of(head * HD, HD), HD)
             for a, slot in enumerate(slots):
-                out_v[slot, :, columns] = mixed[a * BLOCK : (a + 1) * BLOCK]
-        for slot in slots:
-            out_copy(slot).start()
+                rows = pl.ds(pl.multiple_of(block_of(slot) * BLOCK, BLOCK), BLOCK)
+                out[rows, columns] = mixed[a * BLOCK : (a + 1) * BLOCK]
 
     loads[0].wait()
+    loads[1].wait()
     norm()
     pl.semaphore_wait(barrier, len(peers))
     w_far()
     z_first()
-    loads[1].wait()
+    loads[2].wait()
     for j in (1, 2, 3):
         send(ids_v.at[0], ids_v.at[j], 5, i_rs.at[0], x_dev[j])
-    loads[2].wait()
+    loads[3].wait()
 
     def keys(n, carry):
         part = bank_v.at[pl.ds(n * half, half)]
-        pltpu.make_async_copy(part, part, lsem.at[3 + n]).wait()
+        pltpu.make_async_copy(part, part, lsem.at[4 + n]).wait()
         project(0, n)
         pass_on(0, n)
         return carry
 
     lax.fori_loop(0, 2, keys, 0)
-    loads[5].wait()
+    loads[6].wait()
 
     def values(n, carry):
         project(1, n)
@@ -387,7 +391,7 @@
         return carry
 
     lax.fori_loop(0, 2, values, 0)
-    loads[6].wait()
+    loads[7].wait()
     queries(0)
     w_along_y()
     y_step(1, 0)
@@ -395,7 +399,7 @@
     y_step(1, 1)
     neighbour(1)
     landed(ids_v.at[pl.ds(1, 3)], i_rs.at[0])
-    to_smem = pltpu.make_async_copy(ids_v, ids_s, lsem.at[7])
+    to_smem = pltpu.make_async_copy(ids_v, ids_s, lsem.at[8])
     to_smem.start()
     z_step(1, 0)
     w_along_x()
@@ -446,7 +450,10 @@
         return carry
 
     lax.fori_loop(0, 2, serve_near, 0)
+    send_sums(0)
     lax.fori_loop(0, 3, serve_away, 0)
+    send_sums(1)
+    landed(l_in.at[pl.ds(1, 3), 0], l_rs.at[0])
     merge(0, (0, 5))
 
     def merge_near(n, carry):
@@ -458,6 +465,7 @@
         return carry
 
     lax.fori_loop(0, 2, merge_near, 0)
+    landed(l_in.at[pl.ds(1, 3), 1], l_rs.at[1])
     lax.fori_loop(0, 3, merge_away, 0)
 
     for family, like in enumerate((
@@ -473,21 +481,20 @@
         q_in.at[pl.ds(1, 3)],
         q2,
         r_in.at[pl.ds(1, 3)],
+        l_in.at[pl.ds(1, 3)],
     )):
         all_sent(like, family)
-    pltpu.make_async_copy(out_v, out_v, o_sem.at[0]).wait()
 
 
 def per_device(hidden, norm_gain, query_weight, key_weight, value_weight, bank, neighbour_ids):
     hbm = pl.BlockSpec(memory_space=pl.ANY)
-    vmem = pl.BlockSpec(memory_space=pltpu.VMEM)
     dma = pltpu.SemaphoreType.DMA
     width = query_weight.shape[1]
     return pl.pallas_call(
         kernel,
-        out_shape=jax.ShapeDtypeStruct((NZ * BLOCK, width), BF),
-        in_specs=[hbm, vmem, hbm, hbm, hbm, hbm, hbm],
-        out_specs=hbm,
+        out_shape=pltpu.VMEM((NZ * BLOCK, width), BF),
+        in_specs=[hbm] * 7,
+        out_specs=pl.BlockSpec(memory_space=pltpu.VMEM),
         scratch_shapes=[
             pltpu.VMEM((BLOCK, D), BF),
             pltpu.VMEM((D, width), BF),
@@ -501,12 +508,12 @@
             pltpu.VMEM((NZ, 2, BLOCK, HD), BF),
             pltpu.VMEM((HALF, 2, BLOCK, HD), BF),
             pltpu.VMEM((NX, NZ, BLOCK, HD), BF),
-            pltpu.VMEM((NX, HALF, RR, HD), BF),
-            pltpu.VMEM((NX, HALF, RR, HD), BF),
+            pltpu.VMEM((NX, HALF, 2 * BLOCK, HD), BF),
+            pltpu.VMEM((NX, HALF, 2 * BLOCK, HD), BF),
             pltpu.VMEM((NX, 2, NZ), jnp.int32),
             pltpu.SMEM((NX, 2, NZ), jnp.int32),
-            dma((8,)),
-            dma((12,)),
+            dma((9,)),
+            dma((13,)),
             dma((2, 3, 2)),
             dma((2, 4, 4)),
             dma((2,)),
@@ -519,8 +526,10 @@
             dma((2, 2)),
             dma((1,)),
             dma((3,)),
-            pltpu.VMEM((NZ, BLOCK, width), BF),
-            dma((1,)),
+            pltpu.VMEM((1, D), F32),
+            pltpu.VMEM((NX, 2, 8, HD), F32),
+            pltpu.VMEM((NX, 2, 8, HD), F32),
+            dma((2,)),
         ],
         compiler_params=pltpu.CompilerParams(
             collective_id=0, has_side_effects=True, vmem_limit_bytes=56 * 1024 * 1024

time: 86.3 us -> 84.1 us (0.975)
  the two profiles are of different devices: /device:TPU:240 before, /device:TPU:193 now
where the time goes in v5:
time: 84.1 us; the launch traced here: 84 us
  Pallas kernels  83.3 us (99%)
    pallas_call x1, Pallas kernels, per_device(): pl.pallas_call(kernel, out_shape=pltpu.VMEM((NZ * BLOCK, width), BF), in_...  83.3 us

profile of v5, /device:TPU:193, one launch (start us, length us, event | category | flops | bytes accessed | tf_op | source)
XLA Modules:
  0.0 84.0 jit_solution(17908479841724969570)
XLA Ops:
  0.0 83.3 %shard_map.73 = bf16[768,256]{1,0:T(8,128)(2,1)S(1)} custom-call(bf16[64,4096]{1,0:T(8,128)(2,1)} %hidden.1, f32[1,4096]{1,0:T(1,128)} %bitcast.2, bf16[4096,256]{1,0:T(8,128)(2,1)} %wq.1, bf16[4096,256]{1,0:T(8,128)(2,1)} %wk.1, bf16[4096,256]{1,0:T(8,128)(2,1)} %wv.1, bf16[4,128,4096]{2,1,0:T(8,128)(2,1)} %bank.1, s32[2,12]{1,0:T(2,128)} %bitcast.3), custom_call_target="tpu_custom_call" | custom-call | tf_op jit(solution)/shard_map/pallas_call | solution.py:493
  83.3 0.7 copy.9

commit v6 on v5

--- a/solution.py
+++ b/solution.py
@@ -44,12 +44,11 @@
     z_dev = (dev(y, x, c, (z + NZ - turn) % NZ), dev(y, x, c, (z + NZ + turn) % NZ))
     far = dev(y, x, c, (z + HALF) % NZ)
     y_dev = (dev((y + 1) % NY, x, c, z), dev((y + NY - 1) % NY, x, c, z))
-    away = 2 * (y % 2) - 1
-    y_three = tuple(dev((y + NY + away * d) % NY, x, c, z) for d in (1, 2, 3))
+    y_others = tuple(dev((y + d) % NY, x, c, z) for d in (1, 7, 2, 6, 3, 5, 4))
     x_dev = tuple(dev(y, xx, c, z) for xx in xs)
     ring = (dev(y, (x + 1) % NX, c, z), dev(y, (x + NX - 1) % NX, c, z))
     sib = dev(y, x, 1 - c, z)
-    peers = z_dev + (far,) + tuple(dev((y + d) % NY, x, c, z) for d in (1, 2, 3, 5, 6, 7)) + x_dev[1:] + (sib,)
+    peers = z_dev + (far,) + y_others + x_dev[1:] + (sib,)
 
     half = ROWS // 2
     loads = [
@@ -99,15 +98,15 @@
         return w2_v.at[pl.ds(pl.multiple_of(first, 64), count)]
 
     def w_slice(yy):
-        return w_rows(x * 1024 + c * 512 + yy // 2 * 128, 128)
+        return w_rows(x * 1024 + c * 512 + yy * 64, 64)
 
     def w_far():
-        first = pl.multiple_of(x * 1024 + c * 512 + y // 2 * 128, 128)
-        send(wq.at[pl.ds(first, 128)], w_slice(y), 0, w0_rs.at[0], far)
+        first = pl.multiple_of(x * 1024 + c * 512 + y * 64, 64)
+        send(wq.at[pl.ds(first, 64)], w_slice(y), 0, w0_rs.at[0], far)
 
     def w_along_y():
         landed(w_slice(y), w0_rs.at[0])
-        for to in y_three:
+        for to in y_others:
             send(w_slice(y), w_slice(y), 1, wy_rs.at[0], to)
 
     def w_block(xx, cc):
@@ -117,7 +116,7 @@
         return w_rows(xx * 1024 + cc * 512 + half * 256, 256)
 
     def w_along_x():
-        landed(w2_v.at[pl.ds(0, 3 * 128)], wy_rs.at[0])
+        landed(w2_v.at[pl.ds(0, 7 * 64)], wy_rs.at[0])
         own_block = w_block(x, c)
         for way in range(2):
             send(own_block, own_block, 2, wx_rs.at[way, 0], ring[way])
@@ -469,8 +468,8 @@
     lax.fori_loop(0, 3, merge_away, 0)
 
     for family, like in enumerate((
-        w2_v.at[pl.ds(0, 128)],
-        w2_v.at[pl.ds(0, 3 * 128)],
+        w2_v.at[pl.ds(0, 64)],
+        w2_v.at[pl.ds(0, 7 * 64)],
         w2_v.at[pl.ds(0, 1536)],
         w2_v.at[pl.ds(0, D // 2)],
         zb.at[pl.ds(0, 5)],

time: 84.1 us -> 82 us (0.975)
  the two profiles are of different devices: /device:TPU:193 before, /device:TPU:1 now
where the time goes in v6:
time: 82 us; the launch traced here: 81.9 us
  Pallas kernels  81.1 us (99%)
    pallas_call x1, Pallas kernels, per_device(): pl.pallas_call(kernel, out_shape=pltpu.VMEM((NZ * BLOCK, width), BF), in_...  81.1 us

profile of v6, /device:TPU:1, one launch (start us, length us, event | category | flops | bytes accessed | tf_op | source)
XLA Modules:
  0.0 81.9 jit_solution(8023628364416336946)
XLA Ops:
  0.0 81.1 %shard_map.73 = bf16[768,256]{1,0:T(8,128)(2,1)S(1)} custom-call(bf16[64,4096]{1,0:T(8,128)(2,1)} %hidden.1, f32[1,4096]{1,0:T(1,128)} %bitcast.2, bf16[4096,256]{1,0:T(8,128)(2,1)} %wq.1, bf16[4096,256]{1,0:T(8,128)(2,1)} %wk.1, bf16[4096,256]{1,0:T(8,128)(2,1)} %wv.1, bf16[4,128,4096]{2,1,0:T(8,128)(2,1)} %bank.1, s32[2,12]{1,0:T(2,128)} %bitcast.3), custom_call_target="tpu_custom_call" | custom-call | tf_op jit(solution)/shard_map/pallas_call | solution.py:492
  81.1 0.7 copy.9

commit v7 on v6

--- a/solution.py
+++ b/solution.py
@@ -363,11 +363,11 @@
                 rows = pl.ds(pl.multiple_of(block_of(slot) * BLOCK, BLOCK), BLOCK)
                 out[rows, columns] = mixed[a * BLOCK : (a + 1) * BLOCK]
 
+    pl.semaphore_wait(barrier, len(peers))
+    w_far()
     loads[0].wait()
     loads[1].wait()
     norm()
-    pl.semaphore_wait(barrier, len(peers))
-    w_far()
     z_first()
     loads[2].wait()
     for j in (1, 2, 3):

time: 82 us -> 82.4 us (level)
  no operation moved by 1% of the time
where the time goes in v7:
time: 82.4 us; the launch traced here: 82.2 us
  Pallas kernels  81.5 us (99%)
    pallas_call x1, Pallas kernels, per_device(): pl.pallas_call(kernel, out_shape=pltpu.VMEM((NZ * BLOCK, width), BF), in_...  81.5 us

profile of v7, /device:TPU:1, one launch (start us, length us, event | category | flops | bytes accessed | tf_op | source)
XLA Modules:
  0.0 82.2 jit_solution(13820231856228229554)
XLA Ops:
  0.0 81.5 %shard_map.73 = bf16[768,256]{1,0:T(8,128)(2,1)S(1)} custom-call(bf16[64,4096]{1,0:T(8,128)(2,1)} %hidden.1, f32[1,4096]{1,0:T(1,128)} %bitcast.2, bf16[4096,256]{1,0:T(8,128)(2,1)} %wq.1, bf16[4096,256]{1,0:T(8,128)(2,1)} %wk.1, bf16[4096,256]{1,0:T(8,128)(2,1)} %wv.1, bf16[4,128,4096]{2,1,0:T(8,128)(2,1)} %bank.1, s32[2,12]{1,0:T(2,128)} %bitcast.3), custom_call_target="tpu_custom_call" | custom-call | tf_op jit(solution)/shard_map/pallas_call | solution.py:492
  81.5 0.7 copy.9
